TPU v7x, 32 devices: a whole 2x2x4 slice. The times are simulated.
32 devices in a mesh: tile: 32 (over z, y, x, core).
Axes of the slice: x: 2, y: 2, z: 4, core: 2. Of those that a mesh axis runs over, the one named last changes fastest.
Arguments:
- air_state: float32 [8, 256, 128], P(None, 'tile'), may hold values from -6 to 6
- sea_state: float32 [48, 64, 512], P(None, 'tile'), may hold values from -6 to 6
- flux_start: float32 [4, 256, 128], P(None, 'tile'), may hold values from -6 to 6
- air_cells: int32 [32, 5, 1024], P('tile'), may hold values from 0 to 1023
- sea_cells: int32 [32, 5, 1024], P('tile'), may hold values from 0 to 1023
- slot_counts: int32 [32, 5], P('tile'), may hold values from 0 to 1024, as said below
- sea_share: float32 [32, 5, 1024], P('tile'), may hold values from 0.2 to 1
- air_share: float32 [32, 5, 1024], P('tile'), may hold values from 0.2 to 1
- polar_fold_partner: int32 [512], replicated, may hold values from 0 to 511, each once
- wet_mask: int32 [64, 512], P('tile'), may hold values 0 or 1
- air_cotangent: float32 [8, 256, 128], P(None, 'tile'), may hold values from -6 to 6
- sea_cotangent: float32 [48, 64, 512], P(None, 'tile'), may hold values from -6 to 6
- air_encoder: bfloat16 [64, 81], replicated, may hold values from -0.625 to 0.625
- air_depthwise: bfloat16 [64, 9], replicated, may hold values from -2 to 2
- air_expand: bfloat16 [256, 64], replicated, may hold values from -0.75 to 0.75
- air_contract: bfloat16 [64, 256], replicated, may hold values from -0.375 to 0.375
- air_decoder: bfloat16 [12, 64], replicated, may hold values from -0.75 to 0.75
- sea_encoder: bfloat16 [64, 468], replicated, may hold values from -0.25 to 0.25
- sea_depthwise: bfloat16 [64, 9], replicated, may hold values from -2 to 2
- sea_expand: bfloat16 [256, 64], replicated, may hold values from -0.75 to 0.75
- sea_contract: bfloat16 [64, 256], replicated, may hold values from -0.375 to 0.375
- sea_decoder: bfloat16 [48, 64], replicated, may hold values from -0.75 to 0.75
Outputs:
- air_final: float32 [8, 256, 128], P(None, 'tile')
- sea_final: float32 [48, 64, 512], P(None, 'tile')
- air_grad: float32 [8, 256, 128], P(None, 'tile')
- sea_grad: float32 [48, 64, 512], P(None, 'tile')
- flux_grad: float32 [4, 256, 128], P(None, 'tile')
- air_encoder_grad: float32 [64, 81], replicated
- air_depthwise_grad: float32 [64, 9], replicated
- air_expand_grad: float32 [256, 64], replicated
- air_contract_grad: float32 [64, 256], replicated
- air_decoder_grad: float32 [12, 64], replicated
- sea_encoder_grad: float32 [64, 468], replicated
- sea_depthwise_grad: float32 [64, 9], replicated
- sea_expand_grad: float32 [256, 64], replicated
- sea_contract_grad: float32 [64, 256], replicated
- sea_decoder_grad: float32 [48, 64], replicated
Inputs may be any that keep to these rules, and one draw needn't show every extreme that they name: `slot_counts`: the number of used slots of each block, from its first slot on; 0 exactly for blocks whose atmosphere band lies off the grid, at least 256 for all others; in every draw some ocean band has 1024 used slots in every block with an atmosphere band on the grid, and some atmosphere band has 1024 used slots with every ocean band that it is paired with. `air_cells`: a cell of atmosphere band a, numbered row * 128 + column within the band. `sea_cells`: a cell of ocean band o, numbered row * 512 + column within the band. `polar_fold_partner`: each column appears once. `wet_mask`: 1 at ocean cells, 0 on land.
All inputs are finite; a program needn't handle non-finite values. No bound on the sum of `wet_mask` on one device may be relied on, other than what follows from the above.
Results may differ from a plain program's by a relative error of at most 0.025.
Values may be sent and summed in bfloat16 or wider, within the bound.
No kernel may reach another device: no remote copies, remote signals or barrier semaphores. Data moves between devices by JAX's collectives and lax.ppermute only.
A program may use at most 128 MiB of HBM per device.

v0:
```python
from functools import partial
import math

import jax
import jax.numpy as jnp
from jax import lax
from jax.sharding import PartitionSpec as P

STEPS = 2


def passed_along(shard, axis, by):
    length = lax.axis_size(axis)
    pairs = [(i, i + by) for i in range(length) if 0 <= i + by < length]
    return lax.ppermute(shard, axis, pairs)


def with_halo(cells, sides, width):
    for axis, dim in sides:
        count = lax.axis_size(axis)
        ends = count - 1
        head = lax.slice_in_dim(cells, 0, width, axis=dim)
        tail = lax.slice_in_dim(cells, cells.shape[dim] - width, cells.shape[dim], axis=dim)
        cells = jnp.concatenate(
            [
                lax.ppermute(tail, axis, [(i, (i + 1) % count) for i in range(ends)]),
                cells,
                lax.ppermute(head, axis, [((i + 1) % count, i) for i in range(ends)]),
            ],
            axis=dim,
        )
    return cells


def taps(extended):
    rows = extended.shape[1] - 2
    pieces = []
    for shift_row in range(3):
        part = extended[:, shift_row : shift_row + rows]
        for shift_col in (-1, 0, 1):
            pieces.append(jnp.roll(part, -shift_col, axis=2))
    return pieces


def encode(encoder, extended):
    stacked = jnp.concatenate(taps(extended), axis=0)
    inputs, rows, width = stacked.shape
    product = jnp.dot(
        encoder.astype(jnp.bfloat16),
        stacked.reshape(inputs, rows * width),
        preferred_element_type=jnp.float32,
    )
    return product.astype(jnp.bfloat16).reshape(-1, rows, width)


def block(params, padded):
    depthwise, expand, contract, decoder = params
    pieces = taps(padded)
    mixed = pieces[0] * depthwise[:, 0][:, None, None]
    for tap in range(1, 9):
        mixed = mixed + pieces[tap] * depthwise[:, tap][:, None, None]
    channels, rows, width = mixed.shape
    flat = mixed.reshape(channels, rows * width)
    centred = flat - jnp.mean(flat, axis=0, keepdims=True)
    normed = centred * lax.rsqrt(jnp.mean(centred * centred, axis=0, keepdims=True) + 1e-06)
    hidden = jax.nn.gelu(
        jnp.dot(
            expand.astype(jnp.bfloat16),
            normed.astype(jnp.bfloat16),
            preferred_element_type=jnp.float32,
        ),
        approximate=True,
    ).astype(jnp.bfloat16)
    residual = padded[:, 1:-1].reshape(channels, rows * width) + jnp.dot(
        contract.astype(jnp.bfloat16), hidden, preferred_element_type=jnp.float32
    )
    output = jnp.dot(
        decoder.astype(jnp.bfloat16),
        residual.astype(jnp.bfloat16),
        preferred_element_type=jnp.float32,
    )
    return output.reshape(-1, rows, width)


def fold_top(extended, last, partner, width):
    mirrored = jnp.stack([extended[:, -width - 1][:, partner]], axis=1)
    return extended.at[:, -width:].set(jnp.where(last, mirrored, extended[:, -width:]))


def encode_layered(encoder, extended, last, folded, partner):
    if folded:
        extended = fold_top(extended, last, partner, 1)
    return encode(encoder, extended)


def block_layered(params, padded, last, folded, partner):
    if folded:
        padded = fold_top(padded, last, partner, 1)
    return block(params, padded)


def edge_rows(cotangent, width):
    return jnp.concatenate([cotangent[:, :width], cotangent[:, -width:]], axis=1)


def add_rims(inner, returned, width):
    inner = inner.at[:, :width].add(returned[:, :width].astype(jnp.float32))
    return inner.at[:, -width:].add(returned[:, -width:].astype(jnp.float32))


def body(
    air_state,
    sea_state,
    flux_start,
    air_cells,
    sea_cells,
    slot_counts,
    sea_share,
    air_share,
    polar_fold_partner,
    wet_mask,
    air_cotangent,
    sea_cotangent,
    air_encoder,
    air_depthwise,
    air_expand,
    air_contract,
    air_decoder,
    sea_encoder,
    sea_depthwise,
    sea_expand,
    sea_contract,
    sea_decoder,
):
    devices = lax.axis_size("tile")
    position = lax.axis_index("tile")
    last = position == devices - 1
    air_channels = air_state.shape[0]
    sea_channels = sea_state.shape[0]
    flux_channels = flux_start.shape[0]
    air_latitude_total, air_longitude_total = (air_state.shape[1], air_state.shape[2])
    sea_rows, sea_cols = (sea_state.shape[1], sea_state.shape[2])
    atmosphere_exchange_slots = air_cells[0]
    sea_slots = sea_cells[0]
    near_blocks = sea_slots.shape[0]
    centre = (near_blocks - 1) // 2
    slot_count = sea_slots.shape[1]
    used = (jnp.arange(slot_count, dtype=jnp.int32)[None, :] < slot_counts[0][:, None]).astype(
        jnp.float32
    )
    interpolate_to_sky = air_share[0] * used
    toward_sea = sea_share[0] * used
    wet = wet_mask.astype(jnp.float32)

    def route(ocean_blocks, air_blocks, backward):
        at_air = [None] * near_blocks
        at_sea = [None] * near_blocks
        for index in range(near_blocks):
            offset = index - centre
            mirror = near_blocks - 1 - index
            if offset == 0:
                at_air[index] = ocean_blocks[:, index]
                at_sea[index] = air_blocks[:, index]
            else:
                if backward:
                    moved = passed_along(
                        (ocean_blocks[:, index], air_blocks[:, mirror]), "tile", offset
                    )
                else:
                    moved = passed_along(
                        (ocean_blocks[:, index], air_blocks[:, mirror]), "tile", offset
                    )
                at_air[index] = moved[0]
                at_sea[mirror] = moved[1]
        return (jnp.stack(at_air, axis=1), jnp.stack(at_sea, axis=1))

    def forward_model(inputs, weights, folded):
        lowered = inputs.astype(jnp.bfloat16)
        if folded:
            extended = with_halo(lowered, (("tile", 1),), 1)
        else:
            extended = with_halo(lowered, (("tile", 1),), 1)
        encoder_local = partial(
            encode_layered, last=last, folded=folded, partner=polar_fold_partner
        )
        block_local = partial(block_layered, last=last, folded=folded, partner=polar_fold_partner)
        features, encoder_back = jax.vjp(encoder_local, weights[0], extended)
        if folded:
            padded = with_halo(features, (("tile", 1),), 1)
        else:
            padded = with_halo(features, (("tile", 1),), 1)
        outputs, block_back = jax.vjp(block_local, weights[1:], padded.astype(jnp.float32))

        def backward(cotangent):
            block_grads, padded_cotangent = block_back(cotangent)
            if folded:
                returned = with_halo(
                    edge_rows(padded_cotangent, 1).astype(jnp.bfloat16), (("tile", 1),), 1
                ).astype(jnp.float32)
            else:
                returned = with_halo(
                    edge_rows(padded_cotangent, 1).astype(jnp.bfloat16), (("tile", 1),), 1
                ).astype(jnp.float32)
            feature_cotangent = add_rims(padded_cotangent[:, 1:-1], returned, 1)
            encoder_grad, input_cotangent = encoder_back(feature_cotangent.astype(jnp.bfloat16))
            if folded:
                back_in = with_halo(edge_rows(input_cotangent, 1), (("tile", 1),), 1)
            else:
                back_in = with_halo(edge_rows(input_cotangent, 1), (("tile", 1),), 1)
            return (
                (encoder_grad,) + tuple(block_grads),
                add_rims(input_cotangent[:, 1:-1].astype(jnp.float32), back_in, 1),
            )

        return (outputs, backward)

    atmosphere_weight_set = tuple(
        (
            weight.astype(jnp.float32)
            for weight in (air_encoder, air_depthwise, air_expand, air_contract, air_decoder)
        )
    )
    sea_weights = tuple(
        (
            weight.astype(jnp.float32)
            for weight in (sea_encoder, sea_depthwise, sea_expand, sea_contract, sea_decoder)
        )
    )
    air_present_state, sea_now, flux_now = (air_state, sea_state, flux_start)
    record = []
    for step in range(STEPS):
        surface_flat = sea_now[0].reshape(-1)
        flux_flat = flux_now.reshape(flux_channels, -1)
        couple_at_air, couple_at_sea = route(
            (interpolate_to_sky * surface_flat[sea_slots])[None],
            flux_flat[:, atmosphere_exchange_slots],
            False,
        )
        skin_heat_level = (
            jnp.zeros((air_latitude_total * air_longitude_total,), jnp.float32)
            .at[atmosphere_exchange_slots.reshape(-1)]
            .add(couple_at_air[0].reshape(-1))
        )
        inbound_energy_map = (
            jnp.zeros((flux_channels, sea_rows * sea_cols), jnp.float32)
            .at[:, sea_slots.reshape(-1)]
            .add((toward_sea[None] * couple_at_sea).reshape(flux_channels, -1))
        )
        skin_heat_level, inbound_energy_map = (
            skin_heat_level.reshape(air_latitude_total, air_longitude_total),
            inbound_energy_map.reshape(flux_channels, sea_rows, sea_cols),
        )
        air_result_state, air_back = forward_model(
            jnp.concatenate([air_present_state, skin_heat_level[None]], axis=0),
            atmosphere_weight_set,
            False,
        )
        sea_out, sea_back = forward_model(
            jnp.concatenate([sea_now, inbound_energy_map], axis=0), sea_weights, True
        )
        record.append((air_back, sea_back))
        flux_now = air_result_state[air_channels:]
        air_present_state = air_present_state + air_result_state[:air_channels]
        sea_now = sea_now + wet[None] * sea_out
    air_total = tuple((jnp.zeros_like(weight) for weight in atmosphere_weight_set))
    sea_total = tuple((jnp.zeros_like(weight) for weight in sea_weights))
    air_cot = air_cotangent
    sea_cot = sea_cotangent
    flux_cot = jnp.zeros_like(flux_now)
    for step in range(STEPS - 1, -1, -1):
        air_back, sea_back = record[step]
        air_grads, air_inputs = air_back(jnp.concatenate([air_cot, flux_cot], axis=0))
        sea_grads, sea_inputs = sea_back(wet[None] * sea_cot)
        air_total = tuple((total + grad for total, grad in zip(air_total, air_grads)))
        sea_total = tuple((total + grad for total, grad in zip(sea_total, sea_grads)))
        inflow_flat = sea_inputs[sea_channels:].reshape(flux_channels, -1)
        coupler_at_air, coupler_at_sea = route(
            toward_sea[None] * inflow_flat[:, sea_slots],
            air_inputs[air_channels].reshape(-1)[atmosphere_exchange_slots][None],
            True,
        )
        interface_transfer_map = (
            jnp.zeros((sea_rows * sea_cols,), jnp.float32)
            .at[sea_slots.reshape(-1)]
            .add((interpolate_to_sky * coupler_at_sea[0]).reshape(-1))
        )
        fluxes = (
            jnp.zeros((flux_channels, air_latitude_total * air_longitude_total), jnp.float32)
            .at[:, atmosphere_exchange_slots.reshape(-1)]
            .add(coupler_at_air.reshape(flux_channels, -1))
        )
        surface_part = interface_transfer_map.reshape(sea_rows, sea_cols)
        flux_cot = fluxes.reshape(flux_channels, air_latitude_total, air_longitude_total)
        air_cot = air_cot + air_inputs[:air_channels]
        sea_cot = (sea_cot + sea_inputs[:sea_channels]).at[0].add(surface_part)
    summed = lax.psum(air_total + sea_total, "tile")
    air_scale = 1.0 / math.sqrt(air_latitude_total * air_longitude_total * devices)
    sea_scale = 1.0 / math.sqrt(sea_rows * sea_cols * devices)
    return (
        air_present_state,
        sea_now,
        air_cot,
        sea_cot,
        flux_cot,
        summed[0] * air_scale,
        summed[1] * air_scale,
        summed[2] * air_scale,
        summed[3] * air_scale,
        summed[4] * air_scale,
        summed[5] * sea_scale,
        summed[6] * sea_scale,
        summed[7] * sea_scale,
        summed[8] * sea_scale,
        summed[9] * sea_scale,
    )


def solution(mesh):
    placed = (
        P(None, "tile", None),
        P(None, "tile", None),
        P(None, "tile", None),
        P("tile", None, None),
        P("tile", None, None),
        P("tile", None),
        P("tile", None, None),
        P("tile", None, None),
        P(),
        P("tile", None),
        P(None, "tile", None),
        P(None, "tile", None),
        P(),
        P(),
        P(),
        P(),
        P(),
        P(),
        P(),
        P(),
        P(),
        P(),
    )
    return jax.shard_map(
        body,
        mesh=mesh,
        in_specs=placed,
        out_specs=(
            P(None, "tile", None),
            P(None, "tile", None),
            P(None, "tile", None),
            P(None, "tile", None),
            P(None, "tile", None),
            P(),
            P(),
            P(),
            P(),
            P(),
            P(),
            P(),
            P(),
            P(),
            P(),
        ),
        check_vma=False,
    )
```

profile of v0, /device:TPU:0, one launch (start us, length us, event | category | flops | bytes accessed | tf_op | source)
XLA Modules:
  0.0 944.3 jit_solution(4088069769684727740)
XLA Ops:
  10.0 17.7 %gather_fusion.1 = f32[5120,4]{1,0:T(8,128)} fusion(f32[4,1024]{0,1:T(8,128)S(1)} %bitcast.877, s32[5120]{0:T(1024)S(1)} %get-tuple-element.802), kind=kCustom, calls=%fused_computation.1 | custom fusion | bytes 184320 | tf_op jit(solution)/shard_map/gather | solution.py:236
  51.1 28.2 %scatter_custom_fusion.1 = f32[4,1024]{0,1:T(8,128)S(1)} fusion(s32[5120]{0:T(1024)S(1)} %bitcast.1067, f32[5120,4]{1,0:T(8,128)} %copy.571, f32[]{:T(128)} %constant.674.clone.1), kind=kCustom, calls=%fused_computation.347 | custom fusion | flops 20480 | bytes 16896 | tf_op jit(solution)/shard_map/scatter-add | solution.py:247
  98.1 42.0 %gather_fusion = f32[5120]{0:T(1024)} fusion(f32[1024]{0:T(1024)S(1)} %bitcast.859, s32[5120]{0:T(1024)S(1)} %get-tuple-element.803), kind=kCustom, calls=%fused_computation | custom fusion | bytes 61440 | tf_op jit(solution)/shard_map/gather | solution.py:235
  152.3 20.7 %gather_fusion.4 = f32[5120]{0:T(1024)S(1)} fusion(f32[1024]{0:T(1024)S(1)} %bitcast.860, s32[5120]{0:T(1024)S(1)} %get-tuple-element.803), kind=kCustom, calls=%fused_computation.4 | custom fusion | bytes 61440 | tf_op jit(solution)/shard_map/gather | solution.py:235
  190.9 5.4 collective-permute-start.3
  207.2 36.0 %scatter_custom_fusion = f32[1024]{0:T(1024)S(1)} fusion(s32[5120]{0:T(1024)} %bitcast.1071, f32[5120]{0:T(1024)S(1)} %bitcast.1124, f32[]{:T(128)} %constant.674.clone.1), kind=kCustom, calls=%fused_computation.673 | custom fusion | flops 5120 | bytes 4608 | tf_op jit(solution)/shard_map/scatter-add | solution.py:242
  244.7 6.7 collective-permute-start.4
  251.7 36.0 %scatter_custom_fusion.2 = f32[1024]{0:T(1024)S(1)} fusion(s32[5120]{0:T(1024)} %bitcast.1072, f32[5120]{0:T(1024)S(1)} %bitcast.1125, f32[]{:T(128)} %constant.674.clone.1), kind=kCustom, calls=%fused_computation.671 | custom fusion | flops 5120 | bytes 4608 | tf_op jit(solution)/shard_map/scatter-add | solution.py:242
  302.4 6.1 collective-permute-start.20
  308.8 17.7 %gather_fusion.5 = f32[5120,4]{1,0:T(8,128)} fusion(f32[4,1024]{0,1:T(8,128)S(1)} %copy.587, s32[5120]{0:T(1024)S(1)} %get-tuple-element.802), kind=kCustom, calls=%fused_computation.5 | custom fusion | bytes 184320 | tf_op jit(solution)/shard_map/gather | solution.py:236
  332.6 5.7 collective-permute-start.24
  360.0 5.6 collective-permute-start.32
  369.2 28.2 %scatter_custom_fusion.3 = f32[4,1024]{0,1:T(8,128)S(1)} fusion(s32[5120]{0:T(1024)} %bitcast.1068, f32[5120,4]{1,0:T(8,128)} %copy.589, f32[]{:T(128)} %constant.674.clone.1), kind=kCustom, calls=%fused_computation.345 | custom fusion | flops 20480 | bytes 16896 | tf_op jit(solution)/shard_map/scatter-add | solution.py:247
  412.2 20.7 %gather_fusion.9 = f32[5120]{0:T(1024)S(1)} fusion(f32[1024]{0:T(1024)S(1)} %slice_bitcast_fusion.29, s32[5120]{0:T(1024)S(1)} %get-tuple-element.802), kind=kCustom, calls=%fused_computation.9 | custom fusion | bytes 61440 | tf_op jit(solution)/shard_map/gather | solution.py:279
  435.6 5.9 collective-permute-start.28
  444.3 5.1 collective-permute-start.49
  449.5 7.9 collective-permute-start.48
  471.5 36.6 %scatter_custom_fusion.7 = f32[1024]{0:T(1024)} fusion(s32[5120]{0:T(1024)} %bitcast.1069, f32[5120]{0:T(1024)S(1)} %select_multiply_fusion.1, f32[]{:T(128)} %constant.674.clone.1), kind=kCustom, calls=%fused_computation.669 | custom fusion | flops 5120 | bytes 4608 | tf_op jit(solution)/shard_map/scatter-add | solution.py:285
  572.3 6.9 collective-permute-start.38
  606.3 7.0 collective-permute-start.52
  615.1 19.4 %gather_fusion.8 = f32[5120,4]{1,0:T(8,128)} fusion(f32[4,1024]{0,1:T(8,128)S(1)} %copy.630, s32[5120]{0:T(1024)} %copy-done.32), kind=kCustom, calls=%fused_computation.8 | custom fusion | bytes 184320 | tf_op jit(solution)/shard_map/gather | solution.py:278
  660.7 17.7 %gather_fusion.11 = f32[5120,4]{1,0:T(8,128)} fusion(f32[4,1024]{0,1:T(8,128)S(1)} %copy.663, s32[5120]{0:T(1024)S(1)} %copy-done.33), kind=kCustom, calls=%fused_computation.11 | custom fusion | bytes 184320 | tf_op jit(solution)/shard_map/gather | solution.py:278
  686.1 5.0 collective-permute-done.40
  691.2 10.4 %collective-permute-start.43 = (f32[4,1024]{1,0:T(4,128)S(1)}, f32[4,1024]{1,0:T(4,128)S(1)}, u32[]{:S(2)}, u32[]{:S(2)}) collective-permute-start(f32[4,1024]{1,0:T(4,128)S(1)} %get-tuple-element.689), channel_id=1, source_target_pairs={{0,2},{1,3},{2,4},{3,5},{4,6},{5,7},{6,8},{7,9},{8,10},{9,11},{10,... | collective-permute-start | bytes 49160 | tf_op jit(solution)/shard_map/ppermute | solution.py:15
  701.6 5.0 collective-permute-start.42
  718.2 28.5 %scatter_custom_fusion.11 = f32[4,1024]{0,1:T(8,128)S(1)} fusion(s32[5120]{0:T(1024)} %bitcast.1073, f32[5120,4]{1,0:T(8,128)} %copy.665, f32[]{:T(128)} %constant.674.clone.1), kind=kCustom, calls=%fused_computation.341 | custom fusion | flops 20480 | bytes 16896 | tf_op jit(solution)/shard_map/scatter-add | solution.py:290
  749.8 28.2 %scatter_custom_fusion.6 = f32[4,1024]{0,1:T(8,128)S(1)} fusion(s32[5120]{0:T(1024)} %bitcast.1074, f32[5120,4]{1,0:T(8,128)} %copy.632, f32[]{:T(128)} %constant.674.clone.1), kind=kCustom, calls=%fused_computation.343 | custom fusion | flops 20480 | bytes 16896 | tf_op jit(solution)/shard_map/scatter-add | solution.py:290
  785.9 6.3 collective-permute-start.44
  799.5 46.4 %all-reduce.169 = (f32[64,81]{1,0:T(8,128)S(1)}, f32[64,9]{0,1:T(8,128)S(1)}, f32[12,64]{1,0:T(8,128)S(1)}, f32[64,9]{0,1:T(8,128)S(1)}, f32[48,64]{1,0:T(8,128)S(1)}) all-reduce(f32[64,81]{1,0:T(8,128)S(1)} %fusion.51, f32[64,9]{0,1:T(8,128)S(1)} %add_add_fusion.11, f32[12,64]{1,0:T(8,128)S(1)} %fusion.58, ...), channel_id=1, replica_groups=mesh['tile'=32] {'tile'}, use_global_device_ids=true, to_apply=%region_28.29 | all-reduce | flops 10176 | bytes 81408 | tf_op jit(solution)/shard_map/psum | solution.py:296
  856.0 20.7 %gather_fusion.10 = f32[5120]{0:T(1024)S(1)} fusion(f32[1024]{0:T(1024)S(1)} %slice_bitcast_fusion.24, s32[5120]{0:T(1024)S(1)} %copy-done.31), kind=kCustom, calls=%fused_computation.10 | custom fusion | bytes 61440 | tf_op jit(solution)/shard_map/gather | solution.py:279
  879.4 5.3 collective-permute-start.57
  890.5 36.0 %scatter_custom_fusion.10 = f32[1024]{0:T(1024)S(1)} fusion(s32[5120]{0:T(1024)} %bitcast.1070, f32[5120]{0:T(1024)S(1)} %select_multiply_fusion, f32[]{:T(128)} %constant.674.clone.1), kind=kCustom, calls=%fused_computation.667 | custom fusion | flops 5120 | bytes 4608 | tf_op jit(solution)/shard_map/scatter-add | solution.py:285
  (1173 shorter events, 349.0 us)
Async XLA Ops:
  7.3 922.5 %all-reduce.173.cloned.1.call-start = ((), (), s32[]{:S(2)}) async-start(), calls=%async_computation | async-start | bytes 786432 | tf_op jit(solution)/shard_map/psum | solution.py:296
  89.5 50.6 %collective-permute-start.14 = (bf16[64,1,512]{0,2,1:T(8,128)(2,1)S(1)}, bf16[64,1,512]{0,2,1:T(8,128)(2,1)S(1)}, u32[]{:S(2)}, u32[]{:S(2)}) collective-permute-start(bf16[64,1,512]{0,2,1:T(8,128)(2,1)S(1)} %get-tuple-element.616), channel_id=1, source_target_pairs={{0,1},{1,2},{2,3},{3,4},{4,5},{5,6},{6,7},{7,8},{8,9},{9,10},{10,1... | collective-permute-start | bytes 196616 | tf_op jit(solution)/shard_map/ppermute | solution.py:26
  94.0 46.1 %collective-permute-start.15 = (bf16[64,1,512]{0,2,1:T(8,128)(2,1)S(1)}, bf16[64,1,512]{0,2,1:T(8,128)(2,1)S(1)}, u32[]{:S(2)}, u32[]{:S(2)}) collective-permute-start(bf16[64,1,512]{0,2,1:T(8,128)(2,1)S(1)} %get-tuple-element.617), channel_id=1, source_target_pairs={{1,0},{2,1},{3,2},{4,3},{5,4},{6,5},{7,6},{8,7},{9,8},{10,9},{11,1... | collective-permute-start | bytes 196616 | tf_op jit(solution)/shard_map/ppermute | solution.py:28
  173.2 12.9 %collective-permute-start = (f32[1,1024]{1,0:T(1,128)S(1)}, f32[1,1024]{1,0:T(1,128)S(1)}, u32[]{:S(2)}, u32[]{:S(2)}) collective-permute-start(f32[1,1024]{1,0:T(1,128)S(1)} %get-tuple-element.758), channel_id=1, source_target_pairs={{2,0},{3,1},{4,2},{5,3},{6,4},{7,5},{8,6},{9,7},{10,8},{11,9},{12,... | collective-permute-start | bytes 12296 | tf_op jit(solution)/shard_map/ppermute | solution.py:15
  182.2 18.9 %collective-permute-start.17 = (f32[1,1024]{1,0:T(1,128)S(1)}, f32[1,1024]{1,0:T(1,128)S(1)}, u32[]{:S(2)}, u32[]{:S(2)}) collective-permute-start(f32[1,1024]{1,0:T(1,128)S(1)} %get-tuple-element.762), channel_id=1, source_target_pairs={{1,0},{2,1},{3,2},{4,3},{5,4},{6,5},{7,6},{8,7},{9,8},{10,9},{11,1... | collective-permute-start | bytes 12296 | tf_op jit(solution)/shard_map/ppermute | solution.py:15
  183.5 17.6 %collective-permute-start.16 = (f32[1,1024]{1,0:T(1,128)S(1)}, f32[1,1024]{1,0:T(1,128)S(1)}, u32[]{:S(2)}, u32[]{:S(2)}) collective-permute-start(f32[1,1024]{1,0:T(1,128)S(1)} %get-tuple-element.763), channel_id=1, source_target_pairs={{2,0},{3,1},{4,2},{5,3},{6,4},{7,5},{8,6},{9,7},{10,8},{11,9},{12,... | collective-permute-start | bytes 12296 | tf_op jit(solution)/shard_map/ppermute | solution.py:15
  190.9 16.3 %collective-permute-start.3 = (f32[1,1024]{1,0:T(1,128)S(1)}, f32[1,1024]{1,0:T(1,128)S(1)}, u32[]{:S(2)}, u32[]{:S(2)}) collective-permute-start(f32[1,1024]{1,0:T(1,128)S(1)} %get-tuple-element.754), channel_id=1, source_target_pairs={{0,2},{1,3},{2,4},{3,5},{4,6},{5,7},{6,8},{7,9},{8,10},{9,11},{10,... | collective-permute-start | bytes 12296 | tf_op jit(solution)/shard_map/ppermute | solution.py:15
  201.1 50.4 %collective-permute-start.19 = (f32[1,1024]{1,0:T(1,128)S(1)}, f32[1,1024]{1,0:T(1,128)S(1)}, u32[]{:S(2)}, u32[]{:S(2)}) collective-permute-start(f32[1,1024]{1,0:T(1,128)S(1)} %get-tuple-element.759), channel_id=1, source_target_pairs={{0,2},{1,3},{2,4},{3,5},{4,6},{5,7},{6,8},{7,9},{8,10},{9,11},{10,... | collective-permute-start | bytes 12296 | tf_op jit(solution)/shard_map/ppermute | solution.py:15
  205.1 46.3 %collective-permute-start.18 = (f32[1,1024]{1,0:T(1,128)S(1)}, f32[1,1024]{1,0:T(1,128)S(1)}, u32[]{:S(2)}, u32[]{:S(2)}) collective-permute-start(f32[1,1024]{1,0:T(1,128)S(1)} %get-tuple-element.760), channel_id=1, source_target_pairs={{0,1},{1,2},{2,3},{3,4},{4,5},{5,6},{6,7},{7,8},{8,9},{9,10},{10,1... | collective-permute-start | bytes 12296 | tf_op jit(solution)/shard_map/ppermute | solution.py:15
  243.4 44.2 %collective-permute-start.5 = (bf16[9,1,128]{2,0,1:T(8,128)(2,1)S(1)}, bf16[9,1,128]{2,0,1:T(8,128)(2,1)S(1)}, u32[]{:S(2)}, u32[]{:S(2)}) collective-permute-start(bf16[9,1,128]{2,0,1:T(8,128)(2,1)S(1)} %get-tuple-element.748), channel_id=1, source_target_pairs={{1,0},{2,1},{3,2},{4,3},{5,4},{6,5},{7,6},{8,7},{9,8},{10,9},{11,1... | collective-permute-start | bytes 6920 | tf_op jit(solution)/shard_map/ppermute | solution.py:28
  244.7 43.0 %collective-permute-start.4 = (bf16[9,1,128]{2,0,1:T(8,128)(2,1)S(1)}, bf16[9,1,128]{2,0,1:T(8,128)(2,1)S(1)}, u32[]{:S(2)}, u32[]{:S(2)}) collective-permute-start(bf16[9,1,128]{2,0,1:T(8,128)(2,1)S(1)} %get-tuple-element.749), channel_id=1, source_target_pairs={{0,1},{1,2},{2,3},{3,4},{4,5},{5,6},{6,7},{7,8},{8,9},{9,10},{10,1... | collective-permute-start | bytes 6920 | tf_op jit(solution)/shard_map/ppermute | solution.py:26
  301.1 37.4 %collective-permute-start.21 = (bf16[9,1,128]{2,0,1:T(8,128)(2,1)S(1)}, bf16[9,1,128]{2,0,1:T(8,128)(2,1)S(1)}, u32[]{:S(2)}, u32[]{:S(2)}) collective-permute-start(bf16[9,1,128]{2,0,1:T(8,128)(2,1)S(1)} %get-tuple-element.740), channel_id=1, source_target_pairs={{1,0},{2,1},{3,2},{4,3},{5,4},{6,5},{7,6},{8,7},{9,8},{10,9},{11,1... | collective-permute-start | bytes 6920 | tf_op jit(solution)/shard_map/ppermute | solution.py:28
  302.4 36.1 %collective-permute-start.20 = (bf16[9,1,128]{2,0,1:T(8,128)(2,1)S(1)}, bf16[9,1,128]{2,0,1:T(8,128)(2,1)S(1)}, u32[]{:S(2)}, u32[]{:S(2)}) collective-permute-start(bf16[9,1,128]{2,0,1:T(8,128)(2,1)S(1)} %get-tuple-element.741), channel_id=1, source_target_pairs={{0,1},{1,2},{2,3},{3,4},{4,5},{5,6},{6,7},{7,8},{8,9},{9,10},{10,1... | collective-permute-start | bytes 6920 | tf_op jit(solution)/shard_map/ppermute | solution.py:26
  328.9 14.9 %collective-permute-start.25 = (f32[4,1024]{1,0:T(4,128)S(1)}, f32[4,1024]{1,0:T(4,128)S(1)}, u32[]{:S(2)}, u32[]{:S(2)}) collective-permute-start(f32[4,1024]{1,0:T(4,128)S(1)} %get-tuple-element.697), channel_id=1, source_target_pairs={{0,1},{1,2},{2,3},{3,4},{4,5},{5,6},{6,7},{7,8},{8,9},{9,10},{10,1... | collective-permute-start | bytes 49160 | tf_op jit(solution)/shard_map/ppermute | solution.py:15
  343.9 23.0 %collective-permute-start.27 = (f32[4,1024]{1,0:T(4,128)S(1)}, f32[4,1024]{1,0:T(4,128)S(1)}, u32[]{:S(2)}, u32[]{:S(2)}) collective-permute-start(f32[4,1024]{1,0:T(4,128)S(1)} %get-tuple-element.694), channel_id=1, source_target_pairs={{2,0},{3,1},{4,2},{5,3},{6,4},{7,5},{8,6},{9,7},{10,8},{11,9},{12,... | collective-permute-start | bytes 49160 | tf_op jit(solution)/shard_map/ppermute | solution.py:15
  345.2 21.7 %collective-permute-start.26 = (f32[4,1024]{1,0:T(4,128)S(1)}, f32[4,1024]{1,0:T(4,128)S(1)}, u32[]{:S(2)}, u32[]{:S(2)}) collective-permute-start(f32[4,1024]{1,0:T(4,128)S(1)} %get-tuple-element.695), channel_id=1, source_target_pairs={{1,0},{2,1},{3,2},{4,3},{5,4},{6,5},{7,6},{8,7},{9,8},{10,9},{11,1... | collective-permute-start | bytes 49160 | tf_op jit(solution)/shard_map/ppermute | solution.py:15
  360.0 37.6 %collective-permute-start.32 = (bf16[64,1,128]{2,1,0:T(2,128)(2,1)}, bf16[64,1,128]{2,1,0:T(2,128)(2,1)}, u32[]{:S(2)}, u32[]{:S(2)}) collective-permute-start(bf16[64,1,128]{2,1,0:T(2,128)(2,1)} %get-tuple-element.608), channel_id=1, source_target_pairs={{0,1},{1,2},{2,3},{3,4},{4,5},{5,6},{6,7},{7,8},{8,9},{9,10},{10,1... | collective-permute-start | bytes 49160 | tf_op jit(solution)/shard_map/ppermute | solution.py:26
  365.5 32.1 %collective-permute-start.33 = (bf16[64,1,128]{2,1,0:T(2,128)(2,1)}, bf16[64,1,128]{2,1,0:T(2,128)(2,1)}, u32[]{:S(2)}, u32[]{:S(2)}) collective-permute-start(bf16[64,1,128]{2,1,0:T(2,128)(2,1)} %get-tuple-element.609), channel_id=1, source_target_pairs={{1,0},{2,1},{3,2},{4,3},{5,4},{6,5},{7,6},{8,7},{9,8},{10,9},{11,1... | collective-permute-start | bytes 49160 | tf_op jit(solution)/shard_map/ppermute | solution.py:28
  432.9 16.5 %collective-permute-start.51 = (f32[1,1024]{1,0:T(1,128)S(1)}, f32[1,1024]{1,0:T(1,128)S(1)}, u32[]{:S(2)}, u32[]{:S(2)}) collective-permute-start(f32[1,1024]{1,0:T(1,128)S(1)} %get-tuple-element.731), channel_id=1, source_target_pairs={{2,0},{3,1},{4,2},{5,3},{6,4},{7,5},{8,6},{9,7},{10,8},{11,9},{12,... | collective-permute-start | bytes 12296 | tf_op jit(solution)/shard_map/ppermute | solution.py:15
  434.3 24.9 %collective-permute-start.29 = (bf16[52,1,512]{2,0,1:T(8,128)(2,1)S(1)}, bf16[52,1,512]{2,0,1:T(8,128)(2,1)S(1)}, u32[]{:S(2)}, u32[]{:S(2)}) collective-permute-start(bf16[52,1,512]{2,0,1:T(8,128)(2,1)S(1)} %get-tuple-element.681), channel_id=1, source_target_pairs={{1,0},{2,1},{3,2},{4,3},{5,4},{6,5},{7,6},{8,7},{9,8},{10,9},{11,1... | collective-permute-start | bytes 159752 | tf_op jit(solution)/shard_map/ppermute | solution.py:28
  435.6 23.6 %collective-permute-start.28 = (bf16[52,1,512]{2,0,1:T(8,128)(2,1)S(1)}, bf16[52,1,512]{2,0,1:T(8,128)(2,1)S(1)}, u32[]{:S(2)}, u32[]{:S(2)}) collective-permute-start(bf16[52,1,512]{2,0,1:T(8,128)(2,1)S(1)} %get-tuple-element.680), channel_id=1, source_target_pairs={{0,1},{1,2},{2,3},{3,4},{4,5},{5,6},{6,7},{7,8},{8,9},{9,10},{10,1... | collective-permute-start | bytes 159752 | tf_op jit(solution)/shard_map/ppermute | solution.py:26
  443.1 14.9 %collective-permute-start.50 = (f32[1,1024]{1,0:T(1,128)S(1)}, f32[1,1024]{1,0:T(1,128)S(1)}, u32[]{:S(2)}, u32[]{:S(2)}) collective-permute-start(f32[1,1024]{1,0:T(1,128)S(1)} %get-tuple-element.732), channel_id=1, source_target_pairs={{1,0},{2,1},{3,2},{4,3},{5,4},{6,5},{7,6},{8,7},{9,8},{10,9},{11,1... | collective-permute-start | bytes 12296 | tf_op jit(solution)/shard_map/ppermute | solution.py:15
  444.3 13.7 %collective-permute-start.49 = (f32[1,1024]{1,0:T(1,128)S(1)}, f32[1,1024]{1,0:T(1,128)S(1)}, u32[]{:S(2)}, u32[]{:S(2)}) collective-permute-start(f32[1,1024]{1,0:T(1,128)S(1)} %get-tuple-element.734), channel_id=1, source_target_pairs={{0,1},{1,2},{2,3},{3,4},{4,5},{5,6},{6,7},{7,8},{8,9},{9,10},{10,1... | collective-permute-start | bytes 12296 | tf_op jit(solution)/shard_map/ppermute | solution.py:15
  466.4 41.7 %collective-permute-start.30 = (bf16[64,1,512]{0,2,1:T(8,128)(2,1)S(1)}, bf16[64,1,512]{0,2,1:T(8,128)(2,1)S(1)}, u32[]{:S(2)}, u32[]{:S(2)}) collective-permute-start(bf16[64,1,512]{0,2,1:T(8,128)(2,1)S(1)} %get-tuple-element.614), channel_id=1, source_target_pairs={{0,1},{1,2},{2,3},{3,4},{4,5},{5,6},{6,7},{7,8},{8,9},{9,10},{10,1... | collective-permute-start | bytes 196616 | tf_op jit(solution)/shard_map/ppermute | solution.py:26
  470.2 37.9 %collective-permute-start.31 = (bf16[64,1,512]{0,2,1:T(8,128)(2,1)S(1)}, bf16[64,1,512]{0,2,1:T(8,128)(2,1)S(1)}, u32[]{:S(2)}, u32[]{:S(2)}) collective-permute-start(bf16[64,1,512]{0,2,1:T(8,128)(2,1)S(1)} %get-tuple-element.615), channel_id=1, source_target_pairs={{1,0},{2,1},{3,2},{4,3},{5,4},{6,5},{7,6},{8,7},{9,8},{10,9},{11,1... | collective-permute-start | bytes 196616 | tf_op jit(solution)/shard_map/ppermute | solution.py:28
  606.3 31.6 %collective-permute-start.52 = (bf16[64,1,512]{0,2,1:T(8,128)(2,1)S(1)}, bf16[64,1,512]{0,2,1:T(8,128)(2,1)}, u32[]{:S(2)}, u32[]{:S(2)}) collective-permute-start(bf16[64,1,512]{0,2,1:T(8,128)(2,1)S(1)} %get-tuple-element.544), channel_id=1, source_target_pairs={{0,1},{1,2},{2,3},{3,4},{4,5},{5,6},{6,7},{7,8},{8,9},{9,10},{10,1... | collective-permute-start | bytes 196616 | tf_op jit(solution)/shard_map/ppermute | solution.py:26
  613.3 24.5 %collective-permute-start.53 = (bf16[64,1,512]{0,2,1:T(8,128)(2,1)}, bf16[64,1,512]{0,2,1:T(8,128)(2,1)}, u32[]{:S(2)}, u32[]{:S(2)}) collective-permute-start(bf16[64,1,512]{0,2,1:T(8,128)(2,1)} %get-tuple-element.545), channel_id=1, source_target_pairs={{1,0},{2,1},{3,2},{4,3},{5,4},{6,5},{7,6},{8,7},{9,8},{10,9},{11,1... | collective-permute-start | bytes 196616 | tf_op jit(solution)/shard_map/ppermute | solution.py:28
  682.2 24.4 %collective-permute-start.61 = (f32[4,1024]{1,0:T(4,128)S(1)}, f32[4,1024]{1,0:T(4,128)S(1)}, u32[]{:S(2)}, u32[]{:S(2)}) collective-permute-start(f32[4,1024]{1,0:T(4,128)S(1)} %get-tuple-element.687), channel_id=1, source_target_pairs={{1,0},{2,1},{3,2},{4,3},{5,4},{6,5},{7,6},{8,7},{9,8},{10,9},{11,1... | collective-permute-start | bytes 49160 | tf_op jit(solution)/shard_map/ppermute | solution.py:15
  683.5 23.1 %collective-permute-start.60 = (f32[4,1024]{1,0:T(4,128)S(1)}, f32[4,1024]{1,0:T(4,128)S(1)}, u32[]{:S(2)}, u32[]{:S(2)}) collective-permute-start(f32[4,1024]{1,0:T(4,128)S(1)} %get-tuple-element.688), channel_id=1, source_target_pairs={{2,0},{3,1},{4,2},{5,3},{6,4},{7,5},{8,6},{9,7},{10,8},{11,9},{12,... | collective-permute-start | bytes 49160 | tf_op jit(solution)/shard_map/ppermute | solution.py:15
  691.2 56.2 %collective-permute-start.43 = (f32[4,1024]{1,0:T(4,128)S(1)}, f32[4,1024]{1,0:T(4,128)S(1)}, u32[]{:S(2)}, u32[]{:S(2)}) collective-permute-start(f32[4,1024]{1,0:T(4,128)S(1)} %get-tuple-element.689), channel_id=1, source_target_pairs={{0,2},{1,3},{2,4},{3,5},{4,6},{5,7},{6,8},{7,9},{8,10},{9,11},{10,... | collective-permute-start | bytes 49160 | tf_op jit(solution)/shard_map/ppermute | solution.py:15
  701.6 13.4 %collective-permute-start.42 = (f32[4,1024]{1,0:T(4,128)S(1)}, f32[4,1024]{1,0:T(4,128)S(1)}, u32[]{:S(2)}, u32[]{:S(2)}) collective-permute-start(f32[4,1024]{1,0:T(4,128)S(1)} %get-tuple-element.690), channel_id=1, source_target_pairs={{0,1},{1,2},{2,3},{3,4},{4,5},{5,6},{6,7},{7,8},{8,9},{9,10},{10,1... | collective-permute-start | bytes 49160 | tf_op jit(solution)/shard_map/ppermute | solution.py:15
  876.8 13.0 %collective-permute-start.59 = (f32[1,1024]{1,0:T(1,128)S(1)}, f32[1,1024]{1,0:T(1,128)S(1)}, u32[]{:S(2)}, u32[]{:S(2)}) collective-permute-start(f32[1,1024]{1,0:T(1,128)S(1)} %get-tuple-element.726), channel_id=1, source_target_pairs={{2,0},{3,1},{4,2},{5,3},{6,4},{7,5},{8,6},{9,7},{10,8},{11,9},{12,... | collective-permute-start | bytes 12296 | tf_op jit(solution)/shard_map/ppermute | solution.py:15
  (272 other events, 3968.0 us)
Sparse Core Ops, SparseCore 0:
  793.7 136.0 all-reduce.172
where the time goes:
time: 958 us; the launch traced here: 944 us
  other arithmetic  330 us (34%)
  local copies, waits for them, and re-layouts  285 us (30%)
  starting transfers between devices  195 us (20%)
  blocking collectives  46.4 us (5%)
  waiting for transfers between devices  40.1 us (4%)
  matrix products  27.2 us (3%)
  between operations  20.4 us (2%)
    ppermute x32, starting transfers between devices, passed_along(): return lax.ppermute(shard, axis, pairs)  100 us
    ppermute x16, starting transfers between devices, with_halo(): lax.ppermute(tail, axis, [(i, (i + 1) % count) for i in range(ends)])  73.3 us
    scatter-add x2, other arithmetic, body(): interface_transfer_map = jnp.zeros((sea_rows * sea_cols,), jnp.float32).a...  72.6 us
    scatter-add x2, other arithmetic, body(): skin_heat_level = jnp.zeros((air_latitude_total * air_longitude_total,),...  72 us
    gather x2, local copies, waits for them, and re-layouts, body(): surface_flat[sea_slots]  62.8 us
    scatter-add x2, other arithmetic, body(): fluxes = jnp.zeros((flux_channels, air_latitude_total * air_longitude_tot...  56.6 us
    scatter-add x2, other arithmetic, body(): inbound_energy_map = jnp.zeros((flux_channels, sea_rows * sea_cols), jnp....  56.4 us
    psum x1, blocking collectives, body(): summed = lax.psum(air_total + sea_total, 'tile')  46.4 us
  transfers between devices with their start and end apart: 65, of which 16 were waited for; matrix products, arithmetic and copies ran while one was open for 37% of the time, Pallas kernels for 0%

commit v1 on v0

v1 whole, which is shorter than its diff:
```python
import math

import jax
import jax.numpy as jnp
import numpy as np
from jax import lax
from jax.experimental import pallas as pl
from jax.experimental.pallas import tpu as pltpu
from jax.sharding import PartitionSpec as P

F32 = jnp.float32
BF = jnp.bfloat16
OFFS = (-2, -1, 0, 1, 2)
LANE = 128
FORWARD_CHUNK, REPLAY_CHUNK, BACKWARD_CHUNK = 1024, 1024, 1024
VMEM_LIMIT = 16 * 1024 * 1024
SURFACE = 4
CHANNELS = 5


def dot(a, b):
    return lax.dot_general(a, b, (((1,), (0,)), ((), ())), preferred_element_type=F32)


def dot_nt(a, b):
    return lax.dot_general(a, b, (((1,), (1,)), ((), ())), preferred_element_type=F32)


def dot_tn(a, b):
    return lax.dot_general(a, b, (((0,), (0,)), ((), ())), preferred_element_type=F32)


def bf(x):
    return x.astype(BF)


def rounded(x):
    return x.astype(BF).astype(F32)


def iota(shape, axis):
    return lax.broadcasted_iota(jnp.int32, shape, axis)


def load_rows(ref):
    return jnp.concatenate([ref[:, r, :] for r in range(ref.shape[1])], axis=1)


def store_rows(ref, x):
    width = ref.shape[2]
    for r in range(ref.shape[1]):
        ref[:, r, :] = x[:, r * width : (r + 1) * width]


def rolled(x, width, by):
    if by == 0:
        return x
    rows = x.shape[1] // width
    return jnp.concatenate(
        [pltpu.roll(x[:, r * width : (r + 1) * width], (-by) % width, 1) for r in range(rows)], axis=1
    )


def onehot(low):
    return jnp.where(bf(iota((LANE, 1), 0)) == bf(low), jnp.ones((), BF), jnp.zeros((), BF))


def to_table(raw):
    pieces = []
    for ch in range(CHANNELS):
        pieces += [raw[ch : ch + 1, LANE * h : LANE * (h + 1)] for h in range(8)]
    return jnp.concatenate(pieces, axis=0)


def from_table(table):
    rows = []
    for ch in range(table.shape[0] // 8):
        rows.append(jnp.concatenate([table[8 * ch + h : 8 * ch + h + 1] for h in range(8)], axis=1))
    return jnp.concatenate(rows, axis=0) if len(rows) > 1 else rows[0]


def moved(table, path):
    from_hi, from_lo, to_hi, to_lo, weight = path
    gathered = dot(bf(table), onehot(from_lo))
    rows = iota((8, 1), 0).astype(F32)
    picks, puts = rows == from_hi, rows == to_hi
    spread = []
    for g in range(0, table.shape[0], 8):
        value = jnp.sum(jnp.where(picks, gathered[g : g + 8], 0.0), axis=0, keepdims=True) * weight
        spread.append(jnp.where(puts, value, 0.0))
    return dot_nt(bf(jnp.concatenate(spread, axis=0)), onehot(to_lo))


def full_paths(rows, forward):
    line = lambda i: rows[i : i + 1]
    base = 8 if forward else 10
    air = [line(i) for i in range(4)] + [line(base) + line(base + 1)]
    sea = [line(i) for i in range(4, 8)] + [line(base + 4) + line(base + 5)]
    return air, sea


def regrid(paths, tables, forward):
    at_air = at_sea = None
    for (to_air, to_sea), table in zip(paths, tables):
        surface, fluxes = table[8 * SURFACE :], table[: 8 * SURFACE]
        first, second = (surface, fluxes) if forward else (fluxes, surface)
        air = moved(first, to_air)
        sea = moved(second, to_sea)
        at_air = air if at_air is None else at_air + air
        at_sea = sea if at_sea is None else at_sea + sea
    return from_table(at_air), from_table(at_sea)


def own_paths(lists_ref, forward):
    lists = lists_ref[...].astype(F32)
    return [full_paths(lists[16 * d : 16 * d + 16], forward) for d in range(len(OFFS))]


def tables_around(flags_ref, own, near, at_a, at_b):
    own, near, at_a, at_b = [ref[...].astype(F32) for ref in (own, near, at_a, at_b)]
    odd, odd_chip = flags_ref[2] > 0, flags_ref[3] > 0
    up, dn = jnp.where(odd_chip, at_b, at_a), jnp.where(odd_chip, at_a, at_b)
    above = jnp.where(odd, up[48:88], near[0:40])
    below = jnp.where(odd, near[0:40], dn[48:88])
    return [up[0:40], above, own[0:40], below, dn[0:40]]


def couple(paths, tables):
    at_air, at_sea = regrid(paths, tables, True)
    return jnp.concatenate([at_sea, at_air, jnp.zeros((3, at_air.shape[1]), F32)], axis=0)


def sides(near, far, odd):
    return jnp.where(odd, far, near), jnp.where(odd, near, far)


def fold_matrix(partner_ref):
    columns = partner_ref.shape[1]
    return bf(jnp.where(iota((columns, columns), 0) == partner_ref[...], 1.0, 0.0))


def features_of(x, enc_ref, width, flags_ref, fold):
    rows = x.shape[1] // width - 4
    if fold is not None:
        top = x[:, (rows + 1) * width : (rows + 2) * width]
        above = x[:, (rows + 2) * width : (rows + 3) * width]
        above = jnp.where(flags_ref[1] > 0, dot(bf(top), fold), above)
        x = jnp.concatenate([x[:, : (rows + 2) * width], above, x[:, (rows + 3) * width :]], axis=1)
    stack = jnp.concatenate([bf(rolled(x, width, by)) for by in (-1, 0, 1)], axis=0)
    span = (rows + 2) * width
    feat = dot(enc_ref[0], stack[:, 0:span])
    for i in (1, 2):
        feat = feat + dot(enc_ref[i], stack[:, i * width : i * width + span])
    feat = rounded(feat)
    below = jnp.where(flags_ref[0] > 0, 0.0, feat[:, :width])
    above = feat[:, (rows + 1) * width :]
    if fold is not None:
        over = dot(bf(feat[:, rows * width : (rows + 1) * width]), fold)
    else:
        over = 0.0
    above = jnp.where(flags_ref[1] > 0, over, above)
    return stack, jnp.concatenate([below, feat[:, width : (rows + 1) * width], above], axis=1)


def mix(feat, dw_ref, width):
    rows = feat.shape[1] // width - 2
    span = rows * width
    shifted = [rolled(feat, width, by) for by in (-1, 0, 1)]
    total = None
    for i in range(3):
        for j in range(3):
            term = shifted[j][:, i * width : i * width + span] * dw_ref[:, 3 * i + j : 3 * i + j + 1]
            total = term if total is None else total + term
    return total, shifted


def normalise(mixed):
    centred = mixed - jnp.mean(mixed, axis=0, keepdims=True)
    inverse = lax.rsqrt(jnp.mean(centred * centred, axis=0, keepdims=True) + 1e-06)
    return centred * inverse, inverse


GELU_A = math.sqrt(2.0 / math.pi)
GELU_B = 0.044715


def gelu_parts(v):
    square = v * v
    tanh = jnp.tanh(GELU_A * v * (1.0 + GELU_B * square))
    half = 0.5 * (1.0 + tanh)
    return v * half, square, tanh, half


def block_forward(mixed, centre, expand, contract, decoder):
    outs = []
    for c in range(0, mixed.shape[1], FORWARD_CHUNK):
        normed, _ = normalise(mixed[:, c : c + FORWARD_CHUNK])
        hidden = gelu_parts(dot(expand, bf(normed)))[0]
        residual = centre[:, c : c + FORWARD_CHUNK] + dot(contract, bf(hidden))
        outs.append(dot(decoder, bf(residual)))
    return jnp.concatenate(outs, axis=1)


def block_replay(mixed, centre, expand, contract, keep):
    normed_ref, inverse_ref, hid_ref, slope_ref, residual_ref = keep
    for c in range(0, mixed.shape[1], REPLAY_CHUNK):
        at = slice(c, c + REPLAY_CHUNK)
        normed, inverse = normalise(mixed[:, at])
        pre = dot(expand, bf(normed))
        hidden, square, tanh, half = gelu_parts(pre)
        hb = bf(hidden)
        hid_ref[:, at] = hb
        residual_ref[:, at] = bf(centre[:, at] + dot(contract, hb))
        slope = half + (0.5 * GELU_A) * pre * (1.0 - tanh * tanh) * (1.0 + (3.0 * GELU_B) * square)
        slope_ref[:, at] = bf(slope)
        normed_ref[:, at] = normed
        inverse_ref[:, at] = jnp.broadcast_to(inverse, (8, REPLAY_CHUNK))


def block_backward(keep, turned, dy, grow):
    normed_ref, inverse_ref, _, slope_ref, _ = keep
    expand_t, contract_t, decoder_t = turned
    dpre_ref, dres_ref = grow
    dmixes, dress = [], []
    for c in range(0, dy.shape[1], BACKWARD_CHUNK):
        at = slice(c, c + BACKWARD_CHUNK)
        dres_b = bf(dot(decoder_t, bf(dy[:, at])))
        dhid = rounded(dot(contract_t, dres_b))
        dpre = bf(dhid * slope_ref[:, at].astype(F32))
        dn = rounded(dot(expand_t, dpre))
        normed = normed_ref[:, at]
        dmix = inverse_ref[0:1, at] * (
            dn
            - jnp.mean(dn, axis=0, keepdims=True)
            - normed * jnp.mean(dn * normed, axis=0, keepdims=True)
        )
        dpre_ref[:, at] = dpre
        dres_ref[:, at] = dres_b
        dmixes.append(dmix)
        dress.append(dres_b.astype(F32))
    join = lambda parts: jnp.concatenate(parts, axis=1)
    return join(dmixes), join(dress)


def feature_cotangent(dmix, dres, dw_ref, width, flags_ref, fold):
    rows = dres.shape[1] // width
    shifted = [rolled(dmix, width, by) for by in (1, 0, -1)]
    parts = []
    for i in range(3):
        terms = [shifted[j] * dw_ref[:, 3 * i + j : 3 * i + j + 1] for j in range(3)]
        parts.append(terms[0] + terms[1] + terms[2])
    empty = jnp.zeros((dmix.shape[0], width), F32)
    total = jnp.concatenate([parts[0], empty, empty], axis=1)
    total = total + jnp.concatenate([empty, parts[1] + dres, empty], axis=1)
    total = total + jnp.concatenate([empty, empty, parts[2]], axis=1)
    below = jnp.where(flags_ref[0] > 0, 0.0, total[:, :width])
    inner = total[:, width : (rows + 1) * width]
    over = total[:, (rows + 1) * width :]
    if fold is not None:
        back = dot_nt(bf(over), fold)
        top = inner[:, (rows - 1) * width :]
        top = jnp.where(flags_ref[1] > 0, top + back, top)
        inner = jnp.concatenate([inner[:, : (rows - 1) * width], top], axis=1)
    above = jnp.where(flags_ref[1] > 0, 0.0, over)
    return jnp.concatenate([below, inner, above], axis=1)


def input_cotangent(dfeat, enc_t_ref, width, flags_ref, fold):
    rows = dfeat.shape[1] // width - 2
    span = rows * width
    lowered = bf(dfeat)
    spread = None
    for i in range(3):
        start = (2 - i) * width
        term = dot(enc_t_ref[i], lowered[:, start : start + span])
        spread = term if spread is None else spread + term

    def gathered(spread):
        kinds = spread.shape[0] // 3
        parts = [rolled(spread[j * kinds : (j + 1) * kinds], width, 1 - j) for j in range(3)]
        return parts[0] + parts[1] + parts[2]

    dx = gathered(spread)
    if fold is not None:
        over = gathered(dot(enc_t_ref[2], lowered[:, rows * width : (rows + 1) * width]))
        back = dot_nt(bf(over), fold)
        top = dx[:, (rows - 1) * width :]
        top = jnp.where(flags_ref[1] > 0, top + back, top)
        dx = jnp.concatenate([dx[:, : (rows - 1) * width], top], axis=1)
    return dx


def depthwise_terms(dmix, shifted, width):
    span = dmix.shape[1]
    return [
        jnp.sum(dmix * shifted[j][:, i * width : i * width + span], axis=1, keepdims=True)
        for i in range(3)
        for j in range(3)
    ]


def send_edges(dfa, dfs, wa, ws, near, far, odd):
    up = jnp.concatenate([dfa[:, -2 * wa :], dfs[:, -2 * ws :]], axis=1)
    dn = jnp.concatenate([dfa[:, : 2 * wa], dfs[:, : 2 * ws]], axis=1)
    beside, other = sides(up, dn, odd)
    near[...] = bf(beside)
    far[...] = bf(other)


def backward_of(flags_ref, keeps, turned, dys, grows, dws, widths, fold, outs):
    found = []
    for keep, turn, dy, grow, dw, width, matrix, (dy_out, dmix_out, dfeat_out) in zip(
        keeps, turned, dys, grows, dws, widths, (None, fold), outs[0:2]
    ):
        dy_out[...] = bf(dy)
        dmix, dres = block_backward(keep, turn, dy, grow)
        dmix_out[...] = dmix
        dfeat = feature_cotangent(dmix, dres, dw, width, flags_ref, matrix)
        dfeat_out[...] = dfeat
        found.append(dfeat)
    send_edges(*found, *widths, *outs[2], flags_ref[2] > 0)


def weight_terms(air, sea, widths):
    grads = []
    for model in (air, sea):
        normed, hid, residual, dpre, dres = model[0:5]
        grads.append(dot_nt(bf(normed[...]), dpre[...]))
        grads.append(dot_nt(dres[...], hid[...]))
    wa, ws = widths
    dfeat_a, dfeat_s = bf(air[7][...]), bf(sea[7][...])
    air_stack, sea_stack = air[8], sea[8]
    span = dfeat_s.shape[1]
    blank = jnp.zeros((64, 64), F32)
    for i in range(3):
        part = dot_nt(dfeat_s, sea_stack[:, i * ws : i * ws + span])
        grads.append(jnp.concatenate([part, blank], axis=1))
    span = dfeat_a.shape[1]
    nine = jnp.concatenate([air_stack[:, i * wa : i * wa + span] for i in range(3)], axis=0)
    rest = dot_nt(dfeat_a, jnp.concatenate([nine, jnp.zeros((112, span), BF)], axis=0))
    dy_a, dy_s = air[5][...], sea[5][...]
    cells = dy_a.shape[1]
    zero = lambda rows: jnp.zeros((rows, cells), BF)
    rest = rest + dot_nt(air[2][...], jnp.concatenate([zero(144), dy_a, zero(96)], axis=0))
    rest = rest + dot_nt(sea[2][...], jnp.concatenate([zero(160), dy_s, zero(48)], axis=0))
    columns = []
    for model, width in ((air, wa), (sea, ws)):
        feat = model[9][...].astype(F32)
        columns += depthwise_terms(model[6][...], [rolled(feat, width, by) for by in (-1, 0, 1)], width)
    lanes = iota((64, 256), 1)
    for t, column in enumerate(columns):
        rest = rest + jnp.where(lanes == 208 + t, column, 0.0)
    grads.append(rest)
    return grads


def fetch(pairs, sems):
    copies = [pltpu.make_async_copy(src, dst, sems.at[i]) for i, (src, dst) in enumerate(pairs)]
    for copy in copies:
        copy.start()
    for copy in copies:
        copy.wait()


def pack_kernel(flags_ref, *refs):
    sources, outs, held, sems = refs[:8], refs[8:13], refs[13:21], refs[21]
    fetch(list(zip(sources, held)), sems)
    counts_ref, air_ref, sea_ref, flux_ref, ac_ref, sc_ref, ssh_ref, ash_ref = held
    mine, near, far, at_a, at_b = outs
    a = load_rows(air_ref)
    o = load_rows(sea_ref)
    flux = load_rows(flux_ref)
    place = iota((8, LANE), 0) * LANE + iota((8, LANE), 1)
    used = jnp.concatenate([jnp.where(place < counts_ref[0:1, k : k + 1], 1.0, 0.0) for k in range(5)], axis=0)
    ac, sc = ac_ref[...], sc_ref[...]
    wair, wsea = ash_ref[...] * used, ssh_ref[...] * used
    wair_hi, wsea_hi = rounded(wair), rounded(wsea)
    kinds = [
        (ac >> 7).astype(F32), (ac & 127).astype(F32), (sc >> 7).astype(F32), (sc & 127).astype(F32),
        wair_hi, wair - wair_hi, wsea_hi, wsea - wsea_hi,
    ]
    line = lambda x, k: jnp.concatenate([x[8 * k + h : 8 * k + h + 1] for h in range(8)], axis=1)
    air_hi, air_lo, sea_hi, sea_lo, wah, wal, wsh, wsl = [[line(x, k) for k in range(5)] for x in kinds]
    raw = jnp.concatenate([flux, jnp.zeros_like(flux)], axis=0)
    raw = jnp.where(iota((8, 1), 0) == SURFACE, o[0:1], raw)
    heads = []
    for d, off in enumerate(OFFS):
        k, m = 2 + off, 2 - off
        local = [air_hi[k], air_lo[k], sea_hi[m], sea_lo[m], wsh[m], wsl[m], wah[m], wal[m]]
        mine[8 * d : 8 * d + 8] = jnp.concatenate(local, axis=0)
        stat = [sea_hi[k], sea_lo[k], air_hi[m], air_lo[m], wah[k], wal[k], wsh[k], wsl[k]]
        heads.append(jnp.concatenate([raw] + stat, axis=0))
    mine[40:56] = heads[2]
    first, second = sides(heads[4], heads[0], flags_ref[3] > 0)
    at_a[...] = bf(first)
    at_b[...] = bf(second)
    edge = 2 * air_ref.shape[2]
    up = jnp.concatenate([heads[3], band_rows(o, a[:, -edge:])], axis=0)
    dn = jnp.concatenate([heads[1], band_rows(o, a[:, :edge])], axis=0)
    beside, other = sides(up, dn, flags_ref[2] > 0)
    near[...] = bf(beside)
    far[...] = bf(other)


def band_rows(o, a_edge):
    blank = jnp.zeros((8, o.shape[1] - a_edge.shape[1]), F32)
    tail = jnp.concatenate([a_edge, blank], axis=1)
    return jnp.concatenate([o, tail, jnp.zeros_like(tail)], axis=0)


FORMS = {}
for _name, _parts, _rows, _columns in (
    ("aef", 3, 64, 48), ("sef", 3, 64, 192), ("aeb", 3, 48, 64), ("seb", 3, 192, 64),
    ("aex", 1, 256, 64), ("sex", 1, 256, 64), ("aco_t", 1, 256, 64), ("sco_t", 1, 256, 64),
    ("aco", 1, 64, 256), ("sco", 1, 64, 256), ("aex_t", 1, 64, 256), ("sex_t", 1, 64, 256),
    ("ade", 1, 16, 64), ("sde", 1, 48, 64), ("ade_t", 1, 64, 16), ("sde_t", 1, 64, 48),
    ("adw", 1, 64, 9), ("sdw", 1, 64, 9),
):
    _start = max([start + parts * rows for start, parts, rows, _ in FORMS.values()], default=0)
    FORMS[_name] = (_start, _parts, _rows, _columns)
FORM_ROWS = max(start + parts * rows for start, parts, rows, _ in FORMS.values())


def forms(ref, *names):
    found = []
    for name in names:
        start, parts, rows, columns = FORMS[name]
        pieces = [ref[start + rows * i : start + rows * (i + 1), 0:columns] for i in range(parts)]
        if name in ("adw", "sdw"):
            pieces = [piece.astype(F32) for piece in pieces]
        found.append(pieces if parts > 1 else pieces[0])
    return found


def prepare_kernel(*refs):
    sources, out, held, sems = refs[:8], refs[8], refs[9:17], refs[17]
    fetch(list(zip(sources, held)), sems)
    aenc, senc, aex_t, sex_t, aco, sco, sde, small = [ref[...] for ref in held]

    def put(name, value, part=0):
        start, _, rows, columns = FORMS[name]
        out[start + rows * part : start + rows * (part + 1), 0:columns] = bf(value)

    kinds = aenc.shape[1] // 9
    for name, weights, padded in (("a", aenc, 16), ("s", senc, 64)):
        column = iota((1, 3 * padded), 1)
        kind = column % padded
        if name == "a":
            last = kind == kinds - 1 + SURFACE
            kind = jnp.where(kind < kinds - 1, kind, jnp.where(last, kinds - 1, -(1 << 20)))
        else:
            kind = jnp.where(kind < senc.shape[1] // 9, kind, -(1 << 20))
        for i in range(3):
            wanted = (3 * i + column // padded) * (weights.shape[1] // 9) + kind
            picked = dot(weights, bf(jnp.where(iota((weights.shape[1], 1), 0) == wanted, 1.0, 0.0)))
            put(name + "ef", picked, i)
            put(name + "eb", picked.T, i)
    turn = lambda x: x.astype(F32).T
    for name, value in (("aex_t", aex_t), ("sex_t", sex_t), ("aco", aco), ("sco", sco), ("sde", sde)):
        put(name, value)
    for name, value in (("aex", aex_t), ("sex", sex_t), ("aco_t", aco), ("sco_t", sco), ("sde_t", sde)):
        put(name, turn(value))
    small = small.astype(F32)
    put("ade", small[0:16])
    put("ade_t", small[0:16].T)
    put("adw", small[16:32].T[:, 0:9])
    put("sdw", small[32:48].T[:, 0:9])


def couple_kernel(flags_ref, mine, near, far, at_a, at_b, _, lists_out, cpl_out):
    up, dn = sides(near[0:16, :].astype(F32), far[0:16, :].astype(F32), flags_ref[2] > 0)
    up2, dn2 = sides(at_a[...].astype(F32), at_b[...].astype(F32), flags_ref[3] > 0)
    heads = [up2, up, mine[40:56], dn, dn2]
    lists = []
    for d, head in enumerate(heads):
        local = mine[8 * d : 8 * d + 8]
        stat = head[8:16]
        lists.append(
            jnp.concatenate([stat[0:2], local[0:2], stat[2:4], local[2:4], stat[4:8], local[4:8]], axis=0)
        )
    lists_out[...] = bf(jnp.concatenate(lists, axis=0))
    cpl = couple([full_paths(rows, True) for rows in lists], [to_table(head[0:CHANNELS]) for head in heads])
    cpl_out[...] = bf(jnp.concatenate([cpl, jnp.zeros_like(cpl)], axis=0))


def couple_again_kernel(place, lists_ref, own, near, at_a, at_b, a_ref, o_ref, cpl_out, near_out, far_out):
    cpl = couple(own_paths(lists_ref, True), tables_around(place, own, near, at_a, at_b))
    cpl_out[...] = bf(jnp.concatenate([cpl, jnp.zeros_like(cpl)], axis=0))
    a, o = a_ref[...], o_ref[...]
    edge = 2 * LANE
    blank = jnp.zeros((8, o.shape[1] - edge), F32)
    for out, rows in zip((near_out, far_out), sides(a[:, -edge:], a[:, :edge], place[2] > 0)):
        out[0:16, :] = bf(jnp.concatenate([cpl, jnp.concatenate([rows, blank], axis=1)], axis=0))
        out[16:64, :] = bf(o)


def model_inputs(a, o, cpl, bands, cpls):
    edge = 2 * LANE
    rows = iota((8, 1), 0)

    def joined(state_a, state_o, coupled, part):
        air = jnp.where(rows == SURFACE, coupled, 0.0)
        air = air if part is None else air[:, part]
        sea = jnp.where(rows < SURFACE, coupled, 0.0)
        return (
            jnp.concatenate([state_a, air], axis=0),
            jnp.concatenate([state_o, sea, jnp.zeros_like(sea)], axis=0),
        )

    below = joined(bands[0][48:56, :edge], bands[0][0:48], cpls[0], slice(-edge, None))
    above = joined(bands[1][48:56, :edge], bands[1][0:48], cpls[1], slice(0, edge))
    own = joined(a, o, cpl, None)
    return (
        jnp.concatenate([below[0], own[0], above[0]], axis=1),
        jnp.concatenate([below[1], own[1], above[1]], axis=1),
    )


def wet_rows(wet_ref):
    wet = wet_ref[...].astype(F32)
    return jnp.concatenate([wet[r : r + 1] for r in range(wet.shape[0])], axis=1)


def put_table(out, raw):
    out[...] = bf(jnp.concatenate([to_table(raw), jnp.zeros((8, LANE), F32)], axis=0))


def forward_kernel(
    flags_ref, air_ref, o_ref, cpl_ref, band_near, band_far, cpl_near, cpl_far, wet_ref, partner_ref,
    weights_ref, a_out, o_out, table_out, air_stack_out, sea_stack_out, air_feat_out, sea_feat_out,
):
    aef, sef, adw, aex, aco, ade, sdw, sex, sco, sde = forms(
        weights_ref, "aef", "sef", "adw", "aex", "aco", "ade", "sdw", "sex", "sco", "sde"
    )
    wa, ws = LANE, wet_ref.shape[1]
    odd = flags_ref[2] > 0
    a, o = load_rows(air_ref), load_rows(o_ref)
    fold = fold_matrix(partner_ref)
    above, below = sides(band_near[...].astype(F32)[16:80], band_far[...].astype(F32)[16:80], odd)
    cpl_up, cpl_dn = sides(cpl_near[...].astype(F32)[0:8], cpl_far[...].astype(F32)[0:8], odd)
    cpl = cpl_ref[...].astype(F32)[0:8]
    xa, xs = model_inputs(a, o, cpl, (below, above), (cpl_dn, cpl_up))
    air_stack, air_feat = features_of(xa, aef, wa, flags_ref, None)
    sea_stack, sea_feat = features_of(xs, sef, ws, flags_ref, fold)
    air_stack_out[...] = air_stack
    sea_stack_out[...] = sea_stack
    air_feat_out[...] = bf(air_feat)
    sea_feat_out[...] = bf(sea_feat)
    y_air = block_forward(mix(air_feat, adw, wa)[0], air_feat[:, wa:-wa], aex[...], aco[...], ade[...])
    y_sea = block_forward(mix(sea_feat, sdw, ws)[0], sea_feat[:, ws:-ws], sex[...], sco[...], sde[...])
    a = a + y_air[0:8]
    o = o + wet_rows(wet_ref) * y_sea
    a_out[...] = a
    o_out[...] = o
    put_table(table_out, jnp.concatenate([y_air[8:12], o[0:1]], axis=0))


def last_kernel(
    flags_ref, a_ref, o_ref, cpl_ref, band_near, band_far, wet_ref, partner_ref,
    acot_ref, ocot_ref, weights_ref,
    a_out, o_out, air_stack_out, sea_stack_out, air_feat_out, sea_feat_out,
    na, ia, ha, la, ra, ns, is_, hs, ls, rs, pa, ea, ps, es,
    dya, dma, dfa, dys, dms, dfs, near, far,
):
    aef, sef, adw, aex, aco, ade, sdw, sex, sco, sde = forms(
        weights_ref, "aef", "sef", "adw", "aex", "aco", "ade", "sdw", "sex", "sco", "sde"
    )
    aex_t, aco_t, ade_t, sex_t, sco_t, sde_t = forms(weights_ref, "aex_t", "aco_t", "ade_t", "sex_t", "sco_t", "sde_t")
    wa, ws = LANE, wet_ref.shape[1]
    odd = flags_ref[2] > 0
    a, o = a_ref[...], o_ref[...]
    fold = fold_matrix(partner_ref)
    up, dn = sides(band_near[...].astype(F32), band_far[...].astype(F32), odd)
    below, above = [jnp.concatenate([band[16:64], band[8:16]], axis=0) for band in (dn, up)]
    cpl = cpl_ref[...].astype(F32)[0:8]
    xa, xs = model_inputs(a, o, cpl, (below, above), (dn[0:8], up[0:8]))
    air_stack, air_feat = features_of(xa, aef, wa, flags_ref, None)
    sea_stack, sea_feat = features_of(xs, sef, ws, flags_ref, fold)
    air_stack_out[...] = air_stack
    sea_stack_out[...] = sea_stack
    air_feat_out[...] = bf(air_feat)
    sea_feat_out[...] = bf(sea_feat)
    keeps = ((na, ia, ha, la, ra), (ns, is_, hs, ls, rs))
    block_replay(mix(air_feat, adw, wa)[0], air_feat[:, wa:-wa], aex[...], aco[...], keeps[0])
    block_replay(mix(sea_feat, sdw, ws)[0], sea_feat[:, ws:-ws], sex[...], sco[...], keeps[1])
    wet = wet_rows(wet_ref)
    acot = load_rows(acot_ref)
    turned = ((aex_t[...], aco_t[...], ade_t[...]), (sex_t[...], sco_t[...], sde_t[...]))
    backward_of(
        flags_ref, keeps, turned, (jnp.concatenate([acot, jnp.zeros_like(acot)], axis=0), wet * load_rows(ocot_ref)),
        ((pa, ea), (ps, es)), (adw, sdw), (wa, ws), fold, ((dya, dma, dfa), (dys, dms, dfs), (near, far)),
    )
    store_rows(a_out, a + dot(ade[...], ra[...])[0:8])
    store_rows(o_out, o + wet * dot(sde[...], rs[...]))


def replay_kernel(
    air_feat_ref, sea_feat_ref, weights_ref, na, ia, ha, la, ra, ns, is_, hs, ls, rs,
):
    adw, aex, aco, sdw, sex, sco = forms(weights_ref, "adw", "aex", "aco", "sdw", "sex", "sco")
    for feat_ref, dw, ex, co, keep in (
        (air_feat_ref, adw, aex, aco, (na, ia, ha, la, ra)),
        (sea_feat_ref, sdw, sex, sco, (ns, is_, hs, ls, rs)),
    ):
        feat = feat_ref[...].astype(F32)
        width = (feat.shape[1] - na.shape[1]) // 2
        block_replay(mix(feat, dw, width)[0], feat[:, width:-width], ex[...], co[...], keep)


def first_kernel(
    flags_ref, lists_ref, own, t_near, at_a, at_b, acot_ref, ocot_ref, wet_ref, partner_ref,
    na, ia, ha, la, ra, ns, is_, hs, ls, rs, weights_ref,
    ocot_out, pa, ea, ps, es, dya, dma, dfa, dys, dms, dfs, near, far,
):
    adw, sdw = forms(weights_ref, "adw", "sdw")
    aex_t, aco_t, ade_t, sex_t, sco_t, sde_t = forms(weights_ref, "aex_t", "aco_t", "ade_t", "sex_t", "sco_t", "sde_t")
    wa, ws = LANE, wet_ref.shape[1]
    fold = fold_matrix(partner_ref)
    tables = tables_around(flags_ref, own, t_near, at_a, at_b)
    at_air, at_sea = regrid(own_paths(lists_ref, False), tables, False)
    ocot = ocot_ref[...]
    ocot = jnp.where(iota((ocot.shape[0], 1), 0) == 0, ocot + at_sea, ocot)
    ocot_out[...] = ocot
    flux_rows = jnp.concatenate([at_air, jnp.zeros_like(at_air)], axis=0)
    turned = ((aex_t[...], aco_t[...], ade_t[...]), (sex_t[...], sco_t[...], sde_t[...]))
    backward_of(
        flags_ref, ((na, ia, ha, la, ra), (ns, is_, hs, ls, rs)), turned,
        (jnp.concatenate([acot_ref[...], flux_rows], axis=0), wet_rows(wet_ref) * ocot),
        ((pa, ea), (ps, es)), (adw, sdw), (wa, ws), fold, ((dya, dma, dfa), (dys, dms, dfs), (near, far)),
    )


def last_grads_kernel(*refs):
    air, sea, out, done = refs[0:10], refs[10:20], refs[20], refs[21]
    done[...] = jnp.zeros_like(done)
    widths = LANE, (sea[9].shape[1] - sea[0].shape[1]) // 2
    out[...] = jnp.concatenate(weight_terms(air, sea, widths), axis=1)


def first_grads_kernel(*refs):
    air, sea, later, out, done = refs[0:10], refs[10:20], refs[20], refs[22], refs[23]
    done[...] = jnp.zeros_like(done)
    widths = LANE, (sea[9].shape[1] - sea[0].shape[1]) // 2
    for p, grad in enumerate(weight_terms(air, sea, widths)):
        total = bf(later[:, 256 * p : 256 * p + 256] + grad)
        for q in range(4):
            for l in range(2):
                row = 16 * (16 * q + 2 * p + l)
                out[row : row + 16, :] = total[16 * q : 16 * q + 16, LANE * l : LANE * (l + 1)]


def input_kernel(
    flags_ref, dfa_ref, dfs_ref, from_near, from_far, acot_ref, ocot_ref, partner_ref, weights_ref, *refs,
):
    acot_out, ocot_out, table_out = refs[-3:]
    aeb, seb = forms(weights_ref, "aeb", "seb")
    wa, ws = LANE, partner_ref.shape[1]
    fold = fold_matrix(partner_ref)
    up, dn = sides(from_near[...].astype(F32), from_far[...].astype(F32), flags_ref[2] > 0)
    dfa, dfs = dfa_ref[...], dfs_ref[...]
    middle = jnp.zeros((64, dfa.shape[1] - 4 * wa), F32)
    dfa = dfa + jnp.concatenate([dn[:, : 2 * wa], middle, up[:, : 2 * wa]], axis=1)
    dfs = dfs + jnp.concatenate([dn[:, 2 * wa :], up[:, 2 * wa :]], axis=1)
    dxa = input_cotangent(dfa, aeb, wa, flags_ref, None)
    dxs = input_cotangent(dfs, seb, ws, flags_ref, fold)
    if len(acot_ref.shape) == 3:
        acot_out[...] = load_rows(acot_ref) + dxa[0:8]
        ocot_out[...] = load_rows(ocot_ref) + dxs[0:48]
    else:
        store_rows(acot_out, acot_ref[...] + dxa[0:8])
        ocot_out[...] = ocot_ref[...] + dxs[0:48]
    put_table(table_out, jnp.concatenate([dxs[48:52], dxa[12:13]], axis=0))


def total_kernel(terms_ref, _, out):
    total = terms_ref[0].astype(F32)
    for i in range(1, terms_ref.shape[0]):
        total = total + terms_ref[i].astype(F32)
    total = bf(total)
    for i in range(out.shape[0]):
        out[i] = total


def final_kernel(flags_ref, lists_ref, own, near, at_a, at_b, ocot_ref, sea_out, flux_out):
    tables = tables_around(flags_ref, own, near, at_a, at_b)
    at_air, at_sea = regrid(own_paths(lists_ref, False), tables, False)
    ocot = ocot_ref[...]
    ocot = jnp.where(iota((ocot.shape[0], 1), 0) == 0, ocot + at_sea, ocot)
    store_rows(sea_out, ocot)
    store_rows(flux_out, at_air)


def unpack_kernel(
    air_scale, sea_scale, sums_ref, acol_ref, scol_ref, ae, adw, aex, aco, ade, se, sdw, sex, sco, sde,
):
    sums = jnp.concatenate([sums_ref[i].astype(F32) for i in range(sums_ref.shape[0])], axis=0)

    def part(p):
        lanes = []
        for l in range(2):
            rows = [16 * (16 * q + 2 * p + l) for q in range(4)]
            lanes.append(jnp.concatenate([sums[row : row + 16] for row in rows], axis=0))
        return jnp.concatenate(lanes, axis=1)

    aex[...] = part(0) * air_scale
    aco[...] = part(1) * air_scale
    sex[...] = part(2) * sea_scale
    sco[...] = part(3) * sea_scale

    def picked(block, wanted, base):
        chosen = bf(jnp.where(iota((256, wanted.shape[1]), 0) + base == wanted, 1.0, 0.0))
        return dot(bf(block), chosen)

    columns = scol_ref[...]
    se[...] = sea_scale * (picked(part(4), columns, 0) + picked(part(5), columns, 256) + picked(part(6), columns, 512))
    rest = part(7)
    ae[...] = air_scale * picked(rest, acol_ref[...], 0)
    across = rest.T
    adw[...] = air_scale * across[208 : 208 + adw.shape[0]]
    sdw[...] = sea_scale * across[217 : 217 + sdw.shape[0]]
    ade[...] = air_scale * across[144 : 144 + ade.shape[0]]
    sde[...] = sea_scale * across[160 : 160 + sde.shape[0]]


VMEM = pl.BlockSpec(memory_space=pltpu.VMEM)


def place():
    position, count = lax.axis_index("tile"), lax.axis_size("tile")
    return [jnp.int32(0) + x for x in (position == 0, position == count - 1, position % 2, position // 2 % 2)]


def placed_kernel(kernel):
    return lambda *refs: kernel(place(), *refs)


def call(kernel, name, outs, args, scratch=(), specs=None, cost=None, limit=VMEM_LIMIT):
    return pl.pallas_call(
        kernel,
        out_shape=[jax.ShapeDtypeStruct(shape, kind) for shape, kind in outs],
        in_specs=specs or [VMEM] * len(args),
        out_specs=[VMEM] * len(outs),
        scratch_shapes=list(scratch),
        compiler_params=pltpu.CompilerParams(vmem_limit_bytes=limit),
        cost_estimate=cost and pl.CostEstimate(flops=int(cost), bytes_accessed=4 << 20, transcendentals=0),
        name=name,
    )(*args)


def chips_beside(at_a, at_b):
    length = lax.axis_size("tile")
    first = [(i, i ^ 2) for i in range(length)]
    second = [(i, j) for i in range(length) for j in [((i + 2) ^ 2) - 2] if 0 <= j < length]
    at_b = lax.ppermute(at_b, "tile", second)
    return lax.ppermute(at_a, "tile", first), at_b


def beside(near, far):
    length = lax.axis_size("tile")
    chip = [(i, i ^ 1) for i in range(length)]
    other = [(i, j) for i in range(length) for j in [((i + 1) ^ 1) - 1] if 0 <= j < length]
    far = lax.ppermute(far, "tile", other)
    return lax.ppermute(near, "tile", chip), far


def to_all(blocks):
    return lax.all_to_all(blocks, "tile", 0, 0)


def around(table):
    length = lax.axis_size("tile")
    near = lax.ppermute(table, "tile", [(i, i ^ 1) for i in range(length)])
    pair = jnp.concatenate([table, near], axis=0)
    return (table, near, *chips_beside(pair, pair))


def body(
    air_state, sea_state, flux_start, air_cells, sea_cells, slot_counts, sea_share, air_share,
    polar_fold_partner, wet_mask, air_cotangent, sea_cotangent,
    air_encoder, air_depthwise, air_expand, air_contract, air_decoder,
    sea_encoder, sea_depthwise, sea_expand, sea_contract, sea_decoder,
):
    devices = lax.axis_size("tile")
    ach, air_rows, air_width = air_state.shape
    och, sea_rows, sea_width = sea_state.shape
    flux = flux_start.shape[0]
    slots = air_cells.shape[2]
    air_sites, sea_sites = air_rows * air_width, sea_rows * sea_width
    partner = polar_fold_partner.reshape(1, sea_width)

    air_columns, sea_columns = [], []
    for t in range(9):
        i, j = divmod(t, 3)
        air_columns += [48 * i + 16 * j + (k if k < ach else ach + SURFACE) for k in range(ach + 1)]
        sea_columns += [256 * i + 64 * j + k for k in range(och + flux)]
    air_columns, sea_columns = np.array([air_columns], np.int32), np.array([sea_columns], np.int32)

    lines = lambda x: x.reshape(-1, LANE)
    sources = (
        slot_counts, air_state, sea_state, flux_start,
        lines(air_cells), lines(sea_cells), lines(sea_share), lines(air_share),
    )
    head = ((16, sea_sites), BF)
    band = ((80, sea_sites), BF)
    mine, near, far, at_a, at_b = call(
        placed_kernel(pack_kernel), "pack",
        [((56, slots), F32), band, band, head, head],
        sources,
        specs=[pl.BlockSpec(memory_space=pltpu.HBM)] * len(sources),
        limit=60 * 1024 * 1024,
        scratch=[pltpu.VMEM(x.shape, x.dtype) for x in sources] + [pltpu.SemaphoreType.DMA((len(sources),))],
    )
    band_near, band_far = beside(near, far)
    at_a, at_b = chips_beside(at_a, at_b)
    rows_of = lambda x, count: jnp.pad(x, ((0, count - x.shape[0]), (0, 0)))
    small = [rows_of(air_decoder, 16), rows_of(air_depthwise.T, 16), rows_of(sea_depthwise.T, 16)]
    sources = (
        air_encoder, sea_encoder, air_expand.T, sea_expand.T, air_contract, sea_contract, sea_decoder,
        jnp.concatenate(small, axis=0),
    )
    (weights,) = call(
        prepare_kernel, "prepare", [((FORM_ROWS, 256), BF)], sources,
        specs=[pl.BlockSpec(memory_space=pltpu.HBM)] * len(sources), limit=60 * 1024 * 1024, cost=3e9,
        scratch=[pltpu.VMEM(x.shape, x.dtype) for x in sources] + [pltpu.SemaphoreType.DMA((len(sources),))],
    )
    lists, cpl = call(
        placed_kernel(couple_kernel), "couple", [((80, slots), BF), head],
        (mine, band_near, band_far, at_a, at_b, weights),
        specs=[VMEM] * 5 + [pl.BlockSpec(memory_space=pltpu.HBM)],
    )
    cpl_near, cpl_far = beside(cpl, cpl)
    stacks = [((48, (air_rows + 4) * air_width), BF), ((192, (sea_rows + 4) * sea_width), BF)]
    feats = [((64, (air_rows + 2) * air_width), BF), ((64, (sea_rows + 2) * sea_width), BF)]
    keeps, grows, backs = [], [], []
    for sites, outputs, (feat, _) in ((air_sites, 16, feats[0]), (sea_sites, och, feats[1])):
        keeps += [((64, sites), F32), ((8, sites), F32), ((256, sites), BF), ((256, sites), BF), ((64, sites), BF)]
        grows += [((256, sites), BF), ((64, sites), BF)]
        backs += [((outputs, sites), BF), ((64, sites), F32), (feat, F32)]
    halo = ((64, 2 * air_width + 2 * sea_width), BF)
    table = ((48, LANE), BF)
    state = ((64, sea_sites), BF)
    a1, o1, own, ast, sst, aft, sft = call(
        placed_kernel(forward_kernel), "forward",
        [((ach, air_sites), F32), ((och, sea_sites), F32), table, *stacks, *feats],
        (air_state, sea_state, cpl, band_near, band_far, cpl_near, cpl_far, wet_mask, partner, weights),
    )
    cpl, near, far = call(
        placed_kernel(couple_again_kernel), "couple_again", [head, state, state], (lists, *around(own), a1, o1)
    )
    band_near, band_far = beside(near, far)
    air_final, sea_final, ast1, sst1, aft1, sft1, *rest = call(
        placed_kernel(last_kernel), "last",
        [(air_state.shape, F32), (sea_state.shape, F32), *stacks, *feats, *keeps, *grows, *backs, halo, halo],
        (a1, o1, cpl, band_near, band_far, wet_mask, partner, air_cotangent, sea_cotangent,
         weights),
    )
    keep, (pa, ea, ps, es, dya, dma, dfa, dys, dms, dfs, near, far) = rest[:10], rest[10:]
    edge_near, edge_far = beside(near, far)
    gathered = lambda keep, pa, ea, ps, es, dya, dma, dfa, dys, dms, dfs, ast, sst, aft, sft: (
        keep[0], keep[2], keep[4], pa, ea, dya, dma, dfa, ast, aft,
        keep[5], keep[7], keep[9], ps, es, dys, dms, dfs, sst, sft,
    )
    token = ((8, LANE), F32)
    later, done = call(
        last_grads_kernel, "last_grads", [((64, 2048), F32), token],
        gathered(keep, pa, ea, ps, es, dya, dma, dfa, dys, dms, dfs, ast1, sst1, aft1, sft1), cost=3e9,
    )
    acot, ocot, own = call(
        placed_kernel(input_kernel), "inputs", [((ach, air_sites), F32), ((och, sea_sites), F32), table],
        (dfa, dfs, edge_near, edge_far, air_cotangent, sea_cotangent, partner, weights, done),
    )

    keep = call(
        replay_kernel, "replay", keeps, (aft, sft, weights), cost=3e9
    )
    ocot, pa, ea, ps, es, dya, dma, dfa, dys, dms, dfs, near, far = call(
        placed_kernel(first_kernel), "first", [((och, sea_sites), F32), *grows, *backs, halo, halo],
        (lists, *around(own), acot, ocot, wet_mask, partner, *keep, weights),
    )
    edge_near, edge_far = beside(near, far)
    grads, done = call(
        first_grads_kernel, "first_grads", [((8 * LANE, LANE), BF), token],
        (*gathered(keep, pa, ea, ps, es, dya, dma, dfa, dys, dms, dfs, ast, sst, aft, sft), later, edge_near), cost=3e9,
    )
    terms = to_all(grads.reshape(devices, -1, LANE))
    air_grad, ocot, own = call(
        placed_kernel(input_kernel), "first_inputs", [(air_state.shape, F32), ((och, sea_sites), F32), table],
        (dfa, dfs, edge_near, edge_far, acot, ocot, partner, weights, done), cost=5e10,
    )
    tables = around(own)
    (sums,) = call(total_kernel, "total", [(terms.shape, BF)], (terms, tables[2]))
    sums = to_all(sums)
    sea_grad, flux_grad = call(
        placed_kernel(final_kernel), "final", [(sea_state.shape, F32), (flux_start.shape, F32)],
        (lists, *tables, ocot), cost=5e10,
    )
    air_scale = 1.0 / math.sqrt(air_sites * devices)
    sea_scale = 1.0 / math.sqrt(sea_sites * devices)
    flipped = lambda w: (w.shape[1], w.shape[0])
    shapes = [
        air_encoder.shape, flipped(air_depthwise), flipped(air_expand), air_contract.shape, air_decoder.shape,
        sea_encoder.shape, flipped(sea_depthwise), flipped(sea_expand), sea_contract.shape, sea_decoder.shape,
    ]
    ae, dwa, exa, coa, dea, se, dws, exs, cos, des = call(
        lambda *refs: unpack_kernel(air_scale, sea_scale, *refs), "unpack", [(shape, F32) for shape in shapes],
        (sums, air_columns, sea_columns),
    )
    return (
        air_final, sea_final, air_grad, sea_grad, flux_grad,
        ae, dwa.T, exa.T, coa, dea, se, dws.T, exs.T, cos, des,
    )


def solution(mesh):
    rows = P(None, "tile", None)
    blocks = P("tile", None, None)
    placed = (
        (rows,) * 3 + (blocks,) * 2 + (P("tile", None),) + (blocks,) * 2 + (P(), P("tile", None)) + (rows,) * 2 + (P(),) * 10
    )
    return jax.shard_map(
        body, mesh=mesh, in_specs=placed, out_specs=(rows,) * 5 + (P(),) * 10, check_vma=False
    )
```

time: 958 us -> 111 us (0.12); the launches traced: 944 us -> 110 us
  other arithmetic: 330 us -> 1.33 us
  local copies, waits for them, and re-layouts: 285 us -> 3.01 us
  starting transfers between devices: 195 us -> 55.5 us
  blocking collectives: 46.4 us -> 0 us
  Pallas kernels: 0 us -> 31.2 us
  matrix products: 27.2 us -> 0 us
  waiting for transfers between devices: 40.1 us -> 18.4 us
  between operations: 20.4 us -> 0.94 us
    scatter-add x20 -> x0, other arithmetic: 272 us -> none  [the longest x2 72.6 us: body(): interface_transfer_map = jnp.zeros((sea_rows * sea_cols,), jnp.float32).a...]
    gather x18 -> x0, local copies, waits for them, and re-layouts: 192 us -> none  [the longest x2 62.8 us: body(): surface_flat[sea_slots]]
    ppermute x64 -> x21, starting transfers between devices: 195 us -> 42.2 us  [the longest x3 14.5 us: around(): near = lax.ppermute(table, 'tile', [(i, i ^ 1) for i in range(length)])]
    psum x1 -> x0, blocking collectives: 46.4 us -> none  [body(): summed = lax.psum(air_total + sea_total, 'tile')]
    pallas_call x0 -> x15, Pallas kernels: none -> 31.2 us  [call(): pl.pallas_call(kernel, out_shape=[jax.ShapeDtypeStruct(shape, kind) for s...]
    ppermute x64 -> x21, waiting for transfers between devices: 37.8 us -> 7.35 us  [the longest x4 2.88 us: chips_beside(): return (lax.ppermute(at_a, 'tile', first), at_b)]
    dot_general x48 -> x0, matrix products: 27.2 us -> none  [the longest x12 11.3 us: block(): jnp.dot(contract.astype(jnp.bfloat16), hidden, preferred_element_type=jnp...]
    concatenate x21 -> x3, local copies, waits for them, and re-layouts: 26.9 us -> 0.02 us  [around(): pair = jnp.concatenate([table, near], axis=0)]
  transfers between devices with their start and end apart: 65 -> 23, of which waited for: 16 -> 11; matrix products, arithmetic and copies ran while one was open for 37% -> 1% of each run, Pallas kernels for 0% -> 12%
where the time goes in v1:
time: 111 us; the launch traced here: 110 us
  starting transfers between devices  55.5 us (50%)
  Pallas kernels  31.2 us (28%)
  waiting for transfers between devices  18.4 us (17%)
  local copies, waits for them, and re-layouts  3.01 us (3%)
  other arithmetic  1.33 us (1%)
    pallas_call x15, Pallas kernels, call(): pl.pallas_call(kernel, out_shape=[jax.ShapeDtypeStruct(shape, kind) for s...  31.2 us
    ppermute x3, starting transfers between devices, around(): near = lax.ppermute(table, 'tile', [(i, i ^ 1) for i in range(length)])  14.5 us
    all_to_all x2, starting transfers between devices, to_all(): return lax.all_to_all(blocks, 'tile', 0, 0)  13.3 us
    all_to_all x2, waiting for transfers between devices, to_all(): return lax.all_to_all(blocks, 'tile', 0, 0)  11.1 us
    ppermute x4, starting transfers between devices, chips_beside(): return (lax.ppermute(at_a, 'tile', first), at_b)  10.8 us
    ppermute x5, starting transfers between devices, beside(): return (lax.ppermute(near, 'tile', chip), far)  10.8 us
    ppermute x5, starting transfers between devices, beside(): far = lax.ppermute(far, 'tile', other)  3.48 us
    unnamed x29, local copies, waits for them, and re-layouts  2.98 us
  transfers between devices with their start and end apart: 23, of which 11 were waited for; matrix products, arithmetic and copies ran while one was open for 1% of the time, Pallas kernels for 12%

profile of v1, /device:TPU:0, one launch (start us, length us, event | category | flops | bytes accessed | tf_op | source)
XLA Modules:
  0.0 110.4 jit_solution(4927709509377430786)
XLA Ops:
  0.6 2.1 %pack.1 = (f32[56,1024]{1,0:T(8,128)}, bf16[80,1024]{1,0:T(8,128)(2,1)}, bf16[80,1024]{1,0:T(8,128)(2,1)}, bf16[16,1024]{1,0:T(8,128)(2,1)}, bf16[16,1024]{1,0:T(8,128)(2,1)}) custom-call(s32[1,5]{1,0:T(1,128)} %refs_0_.3, f32[8,8,128]{2,1,0:T(8,128)} %refs_0_.5, f32[48,2,512]{2,1,0:T(2,128)} %refs_1_.6, f32[4,8,128]{2,1,0:T(8,128)} %refs_3_.1, ...), custom_call_target="tpu_custom_call" | custom-call | tf_op jit(solution)/shard_map/pack/pallas_call | solution.py:738
  4.0 3.8 %collective-permute-start.2 = (bf16[16,1024]{1,0:T(8,128)(2,1)}, bf16[16,1024]{1,0:T(8,128)(2,1)S(1)}, u32[]{:S(2)}, u32[]{:S(2)}) collective-permute-start(bf16[16,1024]{1,0:T(8,128)(2,1)} %get-tuple-element.104), channel_id=1, source_target_pairs={{0,2},{1,3},{2,0},{3,1},{4,6},{5,7},{6,4},{7,5},{8,10},{9,11},{10,... | collective-permute-start | bytes 98312 | tf_op jit(solution)/shard_map/ppermute | solution.py:755
  8.4 1.3 %fusion.5.refs_7_ = bf16[48,64]{1,0:T(8,128)(2,1)} fusion(bf16[9,64]{1,0:T(8,128)(2,1)} %bitcast.23, bf16[9,64]{1,0:T(8,128)(2,1)} %bitcast.24, bf16[12,64]{1,0:T(8,128)(2,1)} %param.40), kind=kLoop, calls=%fused_computation.15 | loop fusion | flops 43008 | bytes 9984 | tf_op jit(solution)/shard_map/concatenate | solution.py:819
  9.8 2.6 %prepare.1.refs_5_.refs_9_.refs_7_.weights_ref.refs_19_ = bf16[2704,256]{1,0:T(8,128)(2,1)} custom-call(bf16[64,81]{1,0:T(8,128)(2,1)} %refs_0_.4, bf16[64,468]{1,0:T(8,128)(2,1)} %refs_1_.5, bf16[64,256]{1,0:T(8,128)(2,1)} %bitcast.27, bf16[64,256]{1,0:T(8,128)(2,1)} %bitcast.28, bf16[64,256]{1,0:T(8,128)(2,1)} %refs_4_.2, bf16[64,256]{1,0:T(8,128)(2,1)} %refs_5_.3, ...), custom_call_target="tpu_custom_call" | custom-call | flops 3000000000 | bytes 4194304 | tf_op jit(solution)/shard_map/prepare/pallas_call | solution.py:738
  12.8 1.3 %copy-done = bf16[2704,256]{1,0:T(8,128)(2,1)S(1)} copy-done((bf16[2704,256]{1,0:T(8,128)(2,1)S(1)}, bf16[2704,256]{1,0:T(8,128)(2,1)}, u32[]{:S(2)}) %copy-start) | copy-done | bytes 1384472
  14.1 1.4 %couple.1 = (bf16[80,1024]{1,0:T(8,128)(2,1)S(1)}, bf16[16,1024]{1,0:T(8,128)(2,1)S(1)}) custom-call(f32[56,1024]{1,0:T(8,128)S(1)} %copy-done.4, bf16[80,1024]{1,0:T(8,128)(2,1)S(1)} %collective-permute-done.refs_1_.refs_3_, bf16[80,1024]{1,0:T(8,128)(2,1)S(1)} %collective-permute-done.1.refs_2_.refs_4_, ...), custom_call_target="tpu_custom_call" | custom-call | tf_op jit(solution)/shard_map/couple/pallas_call | solution.py:738
  15.5 1.1 collective-permute-start.4
  17.5 2.6 %forward.1 = (f32[8,1024]{1,0:T(8,128)S(1)}, f32[48,1024]{1,0:T(8,128)S(1)}, bf16[48,128]{1,0:T(8,128)(2,1)S(1)}, bf16[48,1536]{1,0:T(8,128)(2,1)S(1)}, bf16[192...) custom-call(f32[8,8,128]{2,1,0:T(8,128)S(1)} %copy-done.6, ...), custom_call_target="tpu_custom_call" | custom-call | tf_op jit(solution)/shard_map/forward/pallas_call | solution.py:738
  20.1 7.0 %collective-permute-start.6 = (bf16[48,128]{1,0:T(8,128)(2,1)S(1)}, bf16[48,128]{1,0:T(8,128)(2,1)S(1)}, u32[]{:S(2)}, u32[]{:S(2)}) collective-permute-start(bf16[48,128]{1,0:T(8,128)(2,1)S(1)} %get-tuple-element.110.refs_1_), channel_id=1, source_target_pairs={{0,1},{1,0},{2,3},{3,2},{4,5},{5,4},{6,7},{7,6},{8,9},{9,8},{10,11... | collective-permute-start | bytes 36872 | tf_op jit(solution)/shard_map/ppermute | solution.py:772
  28.0 2.5 %collective-permute-start.7 = (bf16[96,128]{1,0:T(8,128)(2,1)S(1)}, bf16[96,128]{1,0:T(8,128)(2,1)S(1)}, u32[]{:S(2)}, u32[]{:S(2)}) collective-permute-start(bf16[96,128]{1,0:T(8,128)(2,1)S(1)} %constant_dynamic-update-slice_fusion), channel_id=1, source_target_pairs={{0,2},{1,3},{2,0},{3,1},{4,6},{5,7},{6,4},{7,5},{8,10},{9,11},{10,... | collective-permute-start | bytes 73736 | tf_op jit(solution)/shard_map/ppermute | solution.py:755
  31.1 1.1 %collective-permute-done.7.refs_3_ = bf16[96,128]{1,0:T(8,128)(2,1)S(1)} collective-permute-done((bf16[96,128]{1,0:T(8,128)(2,1)S(1)}, bf16[96,128]{1,0:T(8,128)(2,1)S(1)}, u32[]{:S(2)}, u32[]{:S(2)}) %collective-permute-start.7) | collective-permute-done | bytes 24608 | tf_op jit(solution)/shard_map/ppermute | solution.py:755
  32.3 1.3 %couple_again.1 = (bf16[16,1024]{1,0:T(8,128)(2,1)S(1)}, bf16[64,1024]{1,0:T(8,128)(2,1)S(1)}, bf16[64,1024]{1,0:T(8,128)(2,1)S(1)}) custom-call(bf16[80,1024]{1,0:T(8,128)(2,1)S(1)} %get-tuple-element.109.refs_0_, bf16[48,128]{1,0:T(8,128)(2,1)S(1)} %get-tuple-element.110.refs_1_, bf16[48,128]{1,0:T(8,128)(2,1)S(1)} %collective-permute-done.6.refs_2_, ...), custom_call_target="tpu_custom_call" | custom-call | tf_op jit(solution)/shard_map/couple_again/pallas_call | solution.py:738
  34.3 7.4 %collective-permute-start.9 = (bf16[64,1024]{1,0:T(8,128)(2,1)S(1)}, bf16[64,1024]{1,0:T(8,128)(2,1)S(1)}, u32[]{:S(2)}, u32[]{:S(2)}) collective-permute-start(bf16[64,1024]{1,0:T(8,128)(2,1)S(1)} %get-tuple-element.112), channel_id=1, source_target_pairs={{0,1},{1,0},{2,3},{3,2},{4,5},{5,4},{6,7},{7,6},{8,9},{9,8},{10,11... | collective-permute-start | bytes 393224 | tf_op jit(solution)/shard_map/ppermute | solution.py:763
  41.7 1.0 collective-permute-done.9.refs_3_
  42.7 5.3 %last.1 = (f32[8,8,128]{2,1,0:T(8,128)}, f32[48,2,512]{2,1,0:T(2,128)}, bf16[48,1536]{1,0:T(8,128)(2,1)S(1)}, bf16[192,3072]{1,0:T(8,128)(2,1)S(1)}, bf16[64,128...) custom-call(f32[8,1024]{1,0:T(8,128)S(1)} %get-tuple-element.107.ref, ...), custom_call_target="tpu_custom_call" | custom-call | tf_op jit(solution)/shard_map/last/pallas_call | solution.py:738
  47.9 1.6 %collective-permute-start.11 = (bf16[64,1280]{1,0:T(8,128)(2,1)S(1)}, bf16[64,1280]{1,0:T(8,128)(2,1)S(1)}, u32[]{:S(2)}, u32[]{:S(2)}) collective-permute-start(bf16[64,1280]{1,0:T(8,128)(2,1)S(1)} %get-tuple-element.118), channel_id=1, source_target_pairs={{0,1},{1,0},{2,3},{3,2},{4,5},{5,4},{6,7},{7,6},{8,9},{9,8},{10,11... | collective-permute-start | bytes 491528 | tf_op jit(solution)/shard_map/ppermute | solution.py:763
  50.4 1.9 %last_grads.1 = (f32[64,2048]{1,0:T(8,128)S(1)}, f32[8,128]{1,0:T(8,128)S(1)}) custom-call(f32[64,1024]{1,0:T(8,128)S(1)} %get-tuple-element.120.refs_0_, bf16[256,1024]{1,0:T(8,128)(2,1)S(1)} %get-tuple-element.121.refs_1_, bf16[64,1024]{1,0:T(8,128)(2,1)S(1)} %get-tuple-element.122.refs_2_, bf16[256,1024]{1,0:T(8,128)(2,1)S(1)} %get-tuple-element.123.refs_3_, ...), custom_call_target="tpu_custom_call" | custom-call | flops 3000000000 | bytes 4194304 | tf_op jit(solution)/shard_map/last_grads/pallas_call | solution.py:738
  53.3 7.2 %collective-permute-start.13 = (bf16[48,128]{1,0:T(8,128)(2,1)S(1)}, bf16[48,128]{1,0:T(8,128)(2,1)S(1)}, u32[]{:S(2)}, u32[]{:S(2)}) collective-permute-start(bf16[48,128]{1,0:T(8,128)(2,1)S(1)} %get-tuple-element.139.refs_1_), channel_id=1, source_target_pairs={{0,1},{1,0},{2,3},{3,2},{4,5},{5,4},{6,7},{7,6},{8,9},{9,8},{10,11... | collective-permute-start | bytes 36872 | tf_op jit(solution)/shard_map/ppermute | solution.py:772
  61.3 2.8 %collective-permute-start.14 = (bf16[96,128]{1,0:T(8,128)(2,1)S(1)}, bf16[96,128]{1,0:T(8,128)(2,1)S(1)}, u32[]{:S(2)}, u32[]{:S(2)}) collective-permute-start(bf16[96,128]{1,0:T(8,128)(2,1)S(1)} %constant_dynamic-update-slice_fusion.2), channel_id=1, source_target_pairs={{0,2},{1,3},{2,0},{3,1},{4,6},{5,7},{6,4},{7,5},{8,10},{9,11},{10,... | collective-permute-start | bytes 73736 | tf_op jit(solution)/shard_map/ppermute | solution.py:755
  64.8 2.3 %replay.1 = (f32[64,1024]{1,0:T(8,128)S(1)}, f32[8,1024]{1,0:T(8,128)S(1)}, bf16[256,1024]{1,0:T(8,128)(2,1)S(1)}, bf16[256,1024]{1,0:T(8,128)(2,1)S(1)}, bf16[6...) custom-call(bf16[64,1280]{1,0:T(8,128)(2,1)S(1)} %get-tuple-element., ...), custom_call_target="tpu_custom_call" | custom-call | flops 3000000000 | bytes 4194304 | tf_op jit(solution)/shard_map/replay/pallas_call | solution.py:738
  67.1 2.9 %first.1 = (f32[48,1024]{1,0:T(8,128)S(1)}, bf16[256,1024]{1,0:T(8,128)(2,1)S(1)}, bf16[64,1024]{1,0:T(8,128)(2,1)S(1)}, bf16[256,1024]{1,0:T(8,128)(2,1)S(1)}, ...) custom-call(bf16[80,1024]{1,0:T(8,128)(2,1)S(1)} %get-tuple-element., ...), custom_call_target="tpu_custom_call" | custom-call | tf_op jit(solution)/shard_map/first/pallas_call | solution.py:738
  71.5 2.7 %first_grads.1 = (bf16[1024,128]{1,0:T(8,128)(2,1)}, f32[8,128]{1,0:T(8,128)S(1)}) custom-call(f32[64,1024]{1,0:T(8,128)S(1)} %get-tuple-element.144.refs_9_.refs_0_, bf16[256,1024]{1,0:T(8,128)(2,1)S(1)} %get-tuple-element.146.refs_11_.refs_1_, bf16[64,1024]{1,0:T(8,128)(2,1)S(1)} %get-tuple-element.148.refs_13_.refs_2_, ...), custom_call_target="tpu_custom_call" | custom-call | flops 3000000000 | bytes 4194304 | tf_op jit(solution)/shard_map/first_grads/pallas_call | solution.py:738
  74.2 10.7 %all-to-all-start = ((bf16[32,32,128]{2,1,0:T(8,128)(2,1)}), bf16[32,32,128]{2,1,0:T(8,128)(2,1)S(1)}, u32[]{:S(2)}, u32[]{:S(2)}) async-start(bf16[32,32,128]{2,1,0:T(8,128)(2,1)} %bitcast.9), calls=%async_computation | async-start | bytes 524288 | tf_op jit(solution)/shard_map/all_to_all | solution.py:767
  84.9 1.4 %first_inputs.1 = (f32[8,8,128]{2,1,0:T(8,128)}, f32[48,1024]{1,0:T(8,128)S(1)}, bf16[48,128]{1,0:T(8,128)(2,1)S(1)}) custom-call(f32[64,1280]{1,0:T(8,128)S(1)} %get-tuple-element.154.refs_7_.refs_0_, f32[64,2048]{1,0:T(8,128)S(1)} %get-tuple-element.155.refs_17_.refs_1_, bf16[64,1280]{1,0:T(8,128)(2,1)S(1)} %collective-permute-done.16.refs_21_.refs_2_, ...), custom_call_target="tpu_custom_call" | custom-call | flops 49999998976 | bytes 4194304 | tf_op jit(solution)/shard_map/first_inputs/pallas_call | solution.py:738
  87.3 0.9 collective-permute-done.18.refs_2_
  88.2 1.8 %collective-permute-start.19 = (bf16[96,128]{1,0:T(8,128)(2,1)S(1)}, bf16[96,128]{1,0:T(8,128)(2,1)S(1)}, u32[]{:S(2)}, u32[]{:S(2)}) collective-permute-start(bf16[96,128]{1,0:T(8,128)(2,1)S(1)} %constant_dynamic-update-slice_fusion.4), channel_id=1, source_target_pairs={{0,2},{1,3},{2,0},{3,1},{4,6},{5,7},{6,4},{7,5},{8,10},{9,11},{10,... | collective-permute-start | bytes 73736 | tf_op jit(solution)/shard_map/ppermute | solution.py:755
  90.6 1.4 %collective-permute-done.19.refs_3_._ = bf16[96,128]{1,0:T(8,128)(2,1)S(1)} collective-permute-done((bf16[96,128]{1,0:T(8,128)(2,1)S(1)}, bf16[96,128]{1,0:T(8,128)(2,1)S(1)}, u32[]{:S(2)}, u32[]{:S(2)}) %collective-permute-start.19) | collective-permute-done | bytes 24608 | tf_op jit(solution)/shard_map/ppermute | solution.py:755
  92.0 3.5 %all-to-all-done.terms_ref = bf16[32,32,128]{2,1,0:T(8,128)(2,1)S(1)} async-done(((bf16[32,32,128]{2,1,0:T(8,128)(2,1)}), bf16[32,32,128]{2,1,0:T(8,128)(2,1)S(1)}, u32[]{:S(2)}, u32[]{:S(2)}) %all-to-all-start) | async-done | bytes 262176 | tf_op jit(solution)/shard_map/all_to_all | solution.py:767
  96.3 2.6 %all-to-all-start.1 = ((bf16[32,32,128]{2,1,0:T(8,128)(2,1)}), bf16[32,32,128]{2,1,0:T(8,128)(2,1)S(1)}, u32[]{:S(2)}, u32[]{:S(2)}) async-start(bf16[32,32,128]{2,1,0:T(8,128)(2,1)} %total.1), calls=%async_computation.1 | async-start | bytes 524288 | tf_op jit(solution)/shard_map/all_to_all | solution.py:767
  99.8 2.0 %final.1 = (f32[48,2,512]{2,1,0:T(2,128)}, f32[4,8,128]{2,1,0:T(8,128)}) custom-call(bf16[80,1024]{1,0:T(8,128)(2,1)S(1)} %get-tuple-element.109.refs_0_, bf16[48,128]{1,0:T(8,128)(2,1)S(1)} %get-tuple-element.172.refs_1_, bf16[48,128]{1,0:T(8,128)(2,1)S(1)} %collective-permute-done.18.refs_2_, bf16[96,128]{1,0:T(8,128)(2,1)S(1)} %collective-permute-done.19.refs_3_._, ...), custom_call_target="tpu_custom_call" | custom-call | flops 49999998976 | bytes 4194304 | tf_op jit(solution)/shard_map/final/pallas_call | solution.py:738
  101.8 7.6 %all-to-all-done.1.refs_0_ = bf16[32,32,128]{2,1,0:T(8,128)(2,1)S(1)} async-done(((bf16[32,32,128]{2,1,0:T(8,128)(2,1)}), bf16[32,32,128]{2,1,0:T(8,128)(2,1)S(1)}, u32[]{:S(2)}, u32[]{:S(2)}) %all-to-all-start.1) | async-done | bytes 262176 | tf_op jit(solution)/shard_map/all_to_all | solution.py:767
  109.5 1.0 unpack.1
  (62 shorter events, 13.2 us)
Async XLA Ops:
  2.8 10.0 %collective-permute-start = (bf16[80,1024]{1,0:T(8,128)(2,1)}, bf16[80,1024]{1,0:T(8,128)(2,1)S(1)}, u32[]{:S(2)}, u32[]{:S(2)}) collective-permute-start(bf16[80,1024]{1,0:T(8,128)(2,1)} %get-tuple-element.102), channel_id=1, source_target_pairs={{0,1},{1,0},{2,3},{3,2},{4,5},{5,4},{6,7},{7,6},{8,9},{9,8},{10,11... | collective-permute-start | bytes 491528 | tf_op jit(solution)/shard_map/ppermute | solution.py:763
  3.3 9.5 %collective-permute-start.1 = (bf16[80,1024]{1,0:T(8,128)(2,1)}, bf16[80,1024]{1,0:T(8,128)(2,1)S(1)}, u32[]{:S(2)}, u32[]{:S(2)}) collective-permute-start(bf16[80,1024]{1,0:T(8,128)(2,1)} %get-tuple-element.103), channel_id=1, source_target_pairs={{1,2},{2,1},{3,4},{4,3},{5,6},{6,5},{7,8},{8,7},{9,10},{10,9},{11,... | collective-permute-start | bytes 491528 | tf_op jit(solution)/shard_map/ppermute | solution.py:762
  4.0 8.8 %collective-permute-start.2 = (bf16[16,1024]{1,0:T(8,128)(2,1)}, bf16[16,1024]{1,0:T(8,128)(2,1)S(1)}, u32[]{:S(2)}, u32[]{:S(2)}) collective-permute-start(bf16[16,1024]{1,0:T(8,128)(2,1)} %get-tuple-element.104), channel_id=1, source_target_pairs={{0,2},{1,3},{2,0},{3,1},{4,6},{5,7},{6,4},{7,5},{8,10},{9,11},{10,... | collective-permute-start | bytes 98312 | tf_op jit(solution)/shard_map/ppermute | solution.py:755
  7.8 5.0 %collective-permute-start.3 = (bf16[16,1024]{1,0:T(8,128)(2,1)}, bf16[16,1024]{1,0:T(8,128)(2,1)S(1)}, u32[]{:S(2)}, u32[]{:S(2)}) collective-permute-start(bf16[16,1024]{1,0:T(8,128)(2,1)} %get-tuple-element.105), channel_id=1, source_target_pairs={{2,4},{3,5},{4,2},{5,3},{6,8},{7,9},{8,6},{9,7},{10,12},{11,13},{1... | collective-permute-start | bytes 98312 | tf_op jit(solution)/shard_map/ppermute | solution.py:754
  9.8 7.7 %copy-start.3 = (f32[48,2,512]{2,1,0:T(2,128)S(1)}, f32[48,2,512]{2,1,0:T(2,128)}, u32[]{:S(2)}) copy-start(f32[48,2,512]{2,1,0:T(2,128)} %refs_1_.6) | copy-start | bytes 589828
  9.8 7.7 %copy-start.6 = (f32[8,8,128]{2,1,0:T(8,128)S(1)}, f32[8,8,128]{2,1,0:T(8,128)}, u32[]{:S(2)}) copy-start(f32[8,8,128]{2,1,0:T(8,128)} %refs_0_.5) | copy-start | bytes 98308
  9.8 7.7 %copy-start.7 = (s32[2,512]{1,0:T(2,128)S(1)}, s32[2,512]{1,0:T(2,128)}, u32[]{:S(2)}) copy-start(s32[2,512]{1,0:T(2,128)} %refs_7_.5) | copy-start | bytes 12292
  9.8 7.7 %copy-start.8 = (s32[512]{0:T(512)S(1)}, s32[512]{0:T(512)}, u32[]{:S(2)}) copy-start(s32[512]{0:T(512)} %param.32) | copy-start | bytes 6148
  15.5 2.0 %collective-permute-start.4 = (bf16[16,1024]{1,0:T(8,128)(2,1)S(1)}, bf16[16,1024]{1,0:T(8,128)(2,1)S(1)}, u32[]{:S(2)}, u32[]{:S(2)}) collective-permute-start(bf16[16,1024]{1,0:T(8,128)(2,1)S(1)} %get-tuple-element.106.refs_2_), channel_id=1, source_target_pairs={{0,1},{1,0},{2,3},{3,2},{4,5},{5,4},{6,7},{7,6},{8,9},{9,8},{10,11... | collective-permute-start | bytes 98312 | tf_op jit(solution)/shard_map/ppermute | solution.py:763
  16.6 0.9 collective-permute-start.5
  17.5 25.2 %copy-start.1 = (bf16[2704,256]{1,0:T(8,128)(2,1)S(1)}, bf16[2704,256]{1,0:T(8,128)(2,1)}, u32[]{:S(2)}) copy-start(bf16[2704,256]{1,0:T(8,128)(2,1)} %prepare.1.refs_5_.refs_9_.refs_7_.weights_ref.refs_19_) | copy-start | bytes 4153348
  17.5 25.2 %copy-start.2 = (f32[48,2,512]{2,1,0:T(2,128)S(1)}, f32[48,2,512]{2,1,0:T(2,128)}, u32[]{:S(2)}) copy-start(f32[48,2,512]{2,1,0:T(2,128)} %refs_5_.5) | copy-start | bytes 589828
  17.5 25.2 %copy-start.5 = (f32[8,8,128]{2,1,0:T(8,128)S(1)}, f32[8,8,128]{2,1,0:T(8,128)}, u32[]{:S(2)}) copy-start(f32[8,8,128]{2,1,0:T(8,128)} %refs_4_.3) | copy-start | bytes 98308
  20.1 7.9 %collective-permute-start.6 = (bf16[48,128]{1,0:T(8,128)(2,1)S(1)}, bf16[48,128]{1,0:T(8,128)(2,1)S(1)}, u32[]{:S(2)}, u32[]{:S(2)}) collective-permute-start(bf16[48,128]{1,0:T(8,128)(2,1)S(1)} %get-tuple-element.110.refs_1_), channel_id=1, source_target_pairs={{0,1},{1,0},{2,3},{3,2},{4,5},{5,4},{6,7},{7,6},{8,9},{9,8},{10,11... | collective-permute-start | bytes 36872 | tf_op jit(solution)/shard_map/ppermute | solution.py:772
  28.0 4.3 %collective-permute-start.7 = (bf16[96,128]{1,0:T(8,128)(2,1)S(1)}, bf16[96,128]{1,0:T(8,128)(2,1)S(1)}, u32[]{:S(2)}, u32[]{:S(2)}) collective-permute-start(bf16[96,128]{1,0:T(8,128)(2,1)S(1)} %constant_dynamic-update-slice_fusion), channel_id=1, source_target_pairs={{0,2},{1,3},{2,0},{3,1},{4,6},{5,7},{6,4},{7,5},{8,10},{9,11},{10,... | collective-permute-start | bytes 73736 | tf_op jit(solution)/shard_map/ppermute | solution.py:755
  30.5 1.8 %collective-permute-start.8 = (bf16[96,128]{1,0:T(8,128)(2,1)S(1)}, bf16[96,128]{1,0:T(8,128)(2,1)S(1)}, u32[]{:S(2)}, u32[]{:S(2)}) collective-permute-start(bf16[96,128]{1,0:T(8,128)(2,1)S(1)} %constant_dynamic-update-slice_fusion), channel_id=1, source_target_pairs={{2,4},{3,5},{4,2},{5,3},{6,8},{7,9},{8,6},{9,7},{10,12},{11,13},{1... | collective-permute-start | bytes 73736 | tf_op jit(solution)/shard_map/ppermute | solution.py:754
  33.6 8.1 %collective-permute-start.10 = (bf16[64,1024]{1,0:T(8,128)(2,1)S(1)}, bf16[64,1024]{1,0:T(8,128)(2,1)S(1)}, u32[]{:S(2)}, u32[]{:S(2)}) collective-permute-start(bf16[64,1024]{1,0:T(8,128)(2,1)S(1)} %get-tuple-element.113), channel_id=1, source_target_pairs={{1,2},{2,1},{3,4},{4,3},{5,6},{6,5},{7,8},{8,7},{9,10},{10,9},{11,... | collective-permute-start | bytes 393224 | tf_op jit(solution)/shard_map/ppermute | solution.py:762
  34.3 8.4 %collective-permute-start.9 = (bf16[64,1024]{1,0:T(8,128)(2,1)S(1)}, bf16[64,1024]{1,0:T(8,128)(2,1)S(1)}, u32[]{:S(2)}, u32[]{:S(2)}) collective-permute-start(bf16[64,1024]{1,0:T(8,128)(2,1)S(1)} %get-tuple-element.112), channel_id=1, source_target_pairs={{0,1},{1,0},{2,3},{3,2},{4,5},{5,4},{6,7},{7,6},{8,9},{9,8},{10,11... | collective-permute-start | bytes 393224 | tf_op jit(solution)/shard_map/ppermute | solution.py:763
  47.9 4.4 %collective-permute-start.11 = (bf16[64,1280]{1,0:T(8,128)(2,1)S(1)}, bf16[64,1280]{1,0:T(8,128)(2,1)S(1)}, u32[]{:S(2)}, u32[]{:S(2)}) collective-permute-start(bf16[64,1280]{1,0:T(8,128)(2,1)S(1)} %get-tuple-element.118), channel_id=1, source_target_pairs={{0,1},{1,0},{2,3},{3,2},{4,5},{5,4},{6,7},{7,6},{8,9},{9,8},{10,11... | collective-permute-start | bytes 491528 | tf_op jit(solution)/shard_map/ppermute | solution.py:763
  49.6 2.8 %collective-permute-start.12 = (bf16[64,1280]{1,0:T(8,128)(2,1)S(1)}, bf16[64,1280]{1,0:T(8,128)(2,1)S(1)}, u32[]{:S(2)}, u32[]{:S(2)}) collective-permute-start(bf16[64,1280]{1,0:T(8,128)(2,1)S(1)} %get-tuple-element.119), channel_id=1, source_target_pairs={{1,2},{2,1},{3,4},{4,3},{5,6},{6,5},{7,8},{8,7},{9,10},{10,9},{11,... | collective-permute-start | bytes 491528 | tf_op jit(solution)/shard_map/ppermute | solution.py:762
  53.3 8.0 %collective-permute-start.13 = (bf16[48,128]{1,0:T(8,128)(2,1)S(1)}, bf16[48,128]{1,0:T(8,128)(2,1)S(1)}, u32[]{:S(2)}, u32[]{:S(2)}) collective-permute-start(bf16[48,128]{1,0:T(8,128)(2,1)S(1)} %get-tuple-element.139.refs_1_), channel_id=1, source_target_pairs={{0,1},{1,0},{2,3},{3,2},{4,5},{5,4},{6,7},{7,6},{8,9},{9,8},{10,11... | collective-permute-start | bytes 36872 | tf_op jit(solution)/shard_map/ppermute | solution.py:772
  61.3 5.7 %collective-permute-start.14 = (bf16[96,128]{1,0:T(8,128)(2,1)S(1)}, bf16[96,128]{1,0:T(8,128)(2,1)S(1)}, u32[]{:S(2)}, u32[]{:S(2)}) collective-permute-start(bf16[96,128]{1,0:T(8,128)(2,1)S(1)} %constant_dynamic-update-slice_fusion.2), channel_id=1, source_target_pairs={{0,2},{1,3},{2,0},{3,1},{4,6},{5,7},{6,4},{7,5},{8,10},{9,11},{10,... | collective-permute-start | bytes 73736 | tf_op jit(solution)/shard_map/ppermute | solution.py:755
  64.1 3.0 %collective-permute-start.15 = (bf16[96,128]{1,0:T(8,128)(2,1)S(1)}, bf16[96,128]{1,0:T(8,128)(2,1)S(1)}, u32[]{:S(2)}, u32[]{:S(2)}) collective-permute-start(bf16[96,128]{1,0:T(8,128)(2,1)S(1)} %constant_dynamic-update-slice_fusion.2), channel_id=1, source_target_pairs={{2,4},{3,5},{4,2},{5,3},{6,8},{7,9},{8,6},{9,7},{10,12},{11,13},{1... | collective-permute-start | bytes 73736 | tf_op jit(solution)/shard_map/ppermute | solution.py:754
  70.0 1.5 %collective-permute-start.16 = (bf16[64,1280]{1,0:T(8,128)(2,1)S(1)}, bf16[64,1280]{1,0:T(8,128)(2,1)S(1)}, u32[]{:S(2)}, u32[]{:S(2)}) collective-permute-start(bf16[64,1280]{1,0:T(8,128)(2,1)S(1)} %get-tuple-element.156), channel_id=1, source_target_pairs={{0,1},{1,0},{2,3},{3,2},{4,5},{5,4},{6,7},{7,6},{8,9},{9,8},{10,11... | collective-permute-start | bytes 491528 | tf_op jit(solution)/shard_map/ppermute | solution.py:763
  70.1 14.8 %collective-permute-start.17 = (bf16[64,1280]{1,0:T(8,128)(2,1)S(1)}, bf16[64,1280]{1,0:T(8,128)(2,1)S(1)}, u32[]{:S(2)}, u32[]{:S(2)}) collective-permute-start(bf16[64,1280]{1,0:T(8,128)(2,1)S(1)} %get-tuple-element.157), channel_id=1, source_target_pairs={{1,2},{2,1},{3,4},{4,3},{5,6},{6,5},{7,8},{8,7},{9,10},{10,9},{11,... | collective-permute-start | bytes 491528 | tf_op jit(solution)/shard_map/ppermute | solution.py:762
  74.2 21.3 %all-to-all-start = ((bf16[32,32,128]{2,1,0:T(8,128)(2,1)}), bf16[32,32,128]{2,1,0:T(8,128)(2,1)S(1)}, u32[]{:S(2)}, u32[]{:S(2)}) async-start(bf16[32,32,128]{2,1,0:T(8,128)(2,1)} %bitcast.9), calls=%async_computation | async-start | bytes 524288 | tf_op jit(solution)/shard_map/all_to_all | solution.py:767
  87.0 1.2 %collective-permute-start.18 = (bf16[48,128]{1,0:T(8,128)(2,1)S(1)}, bf16[48,128]{1,0:T(8,128)(2,1)S(1)}, u32[]{:S(2)}, u32[]{:S(2)}) collective-permute-start(bf16[48,128]{1,0:T(8,128)(2,1)S(1)} %get-tuple-element.172.refs_1_), channel_id=1, source_target_pairs={{0,1},{1,0},{2,3},{3,2},{4,5},{5,4},{6,7},{7,6},{8,9},{9,8},{10,11... | collective-permute-start | bytes 36872 | tf_op jit(solution)/shard_map/ppermute | solution.py:772
  88.2 3.8 %collective-permute-start.19 = (bf16[96,128]{1,0:T(8,128)(2,1)S(1)}, bf16[96,128]{1,0:T(8,128)(2,1)S(1)}, u32[]{:S(2)}, u32[]{:S(2)}) collective-permute-start(bf16[96,128]{1,0:T(8,128)(2,1)S(1)} %constant_dynamic-update-slice_fusion.4), channel_id=1, source_target_pairs={{0,2},{1,3},{2,0},{3,1},{4,6},{5,7},{6,4},{7,5},{8,10},{9,11},{10,... | collective-permute-start | bytes 73736 | tf_op jit(solution)/shard_map/ppermute | solution.py:755
  90.0 8.9 %collective-permute-start.20 = (bf16[96,128]{1,0:T(8,128)(2,1)S(1)}, bf16[96,128]{1,0:T(8,128)(2,1)S(1)}, u32[]{:S(2)}, u32[]{:S(2)}) collective-permute-start(bf16[96,128]{1,0:T(8,128)(2,1)S(1)} %constant_dynamic-update-slice_fusion.4), channel_id=1, source_target_pairs={{2,4},{3,5},{4,2},{5,3},{6,8},{7,9},{8,6},{9,7},{10,12},{11,13},{1... | collective-permute-start | bytes 73736 | tf_op jit(solution)/shard_map/ppermute | solution.py:754
  96.3 13.2 %all-to-all-start.1 = ((bf16[32,32,128]{2,1,0:T(8,128)(2,1)}), bf16[32,32,128]{2,1,0:T(8,128)(2,1)S(1)}, u32[]{:S(2)}, u32[]{:S(2)}) async-start(bf16[32,32,128]{2,1,0:T(8,128)(2,1)} %total.1), calls=%async_computation.1 | async-start | bytes 524288 | tf_op jit(solution)/shard_map/all_to_all | solution.py:767
  99.8 9.7 %copy-start.9 = (s32[1,468]{1,0:T(1,128)S(1)}, s32[1,468]{1,0:T(1,128)}, u32[]{:S(2)}) copy-start(s32[1,468]{1,0:T(1,128)} %constant.8.clone.refs_2_) | copy-start | bytes 5620
  99.8 9.7 %copy-start.10 = (s32[1,81]{1,0:T(1,128)S(1)}, s32[1,81]{1,0:T(1,128)}, u32[]{:S(2)}) copy-start(s32[1,81]{1,0:T(1,128)} %constant.7.clone.refs_1_) | copy-start | bytes 976
  (4 other events, 6.0 us)

commit v2 on v1

--- a/solution.py
+++ b/solution.py
@@ -217,17 +217,17 @@
         inverse_ref[:, at] = jnp.broadcast_to(inverse, (8, REPLAY_CHUNK))
 
 
-def block_backward(keep, turned, dy, grow):
+def block_backward(keep, weights, dy, grow):
     normed_ref, inverse_ref, _, slope_ref, _ = keep
-    expand_t, contract_t, decoder_t = turned
+    expand, contract, decoder = weights
     dpre_ref, dres_ref = grow
     dmixes, dress = [], []
     for c in range(0, dy.shape[1], BACKWARD_CHUNK):
         at = slice(c, c + BACKWARD_CHUNK)
-        dres_b = bf(dot(decoder_t, bf(dy[:, at])))
-        dhid = rounded(dot(contract_t, dres_b))
+        dres_b = bf(dot_tn(decoder, bf(dy[:, at])))
+        dhid = rounded(dot_tn(contract, dres_b))
         dpre = bf(dhid * slope_ref[:, at].astype(F32))
-        dn = rounded(dot(expand_t, dpre))
+        dn = rounded(dot_tn(expand, dpre))
         normed = normed_ref[:, at]
         dmix = inverse_ref[0:1, at] * (
             dn
@@ -265,14 +265,14 @@
     return jnp.concatenate([below, inner, above], axis=1)
 
 
-def input_cotangent(dfeat, enc_t_ref, width, flags_ref, fold):
+def input_cotangent(dfeat, enc_ref, width, flags_ref, fold):
     rows = dfeat.shape[1] // width - 2
     span = rows * width
     lowered = bf(dfeat)
     spread = None
     for i in range(3):
         start = (2 - i) * width
-        term = dot(enc_t_ref[i], lowered[:, start : start + span])
+        term = dot_tn(enc_ref[i], lowered[:, start : start + span])
         spread = term if spread is None else spread + term
 
     def gathered(spread):
@@ -282,7 +282,7 @@
 
     dx = gathered(spread)
     if fold is not None:
-        over = gathered(dot(enc_t_ref[2], lowered[:, rows * width : (rows + 1) * width]))
+        over = gathered(dot_tn(enc_ref[2], lowered[:, rows * width : (rows + 1) * width]))
         back = dot_nt(bf(over), fold)
         top = dx[:, (rows - 1) * width :]
         top = jnp.where(flags_ref[1] > 0, top + back, top)
@@ -290,10 +290,10 @@
     return dx
 
 
-def depthwise_terms(dmix, shifted, width):
-    span = dmix.shape[1]
+def depthwise_terms(shifted, feat, width):
+    span = shifted[0].shape[1]
     return [
-        jnp.sum(dmix * shifted[j][:, i * width : i * width + span], axis=1, keepdims=True)
+        jnp.sum(shifted[j] * feat[:, i * width : i * width + span], axis=1, keepdims=True)
         for i in range(3)
         for j in range(3)
     ]
@@ -307,10 +307,10 @@
     far[...] = bf(other)
 
 
-def backward_of(flags_ref, keeps, turned, dys, grows, dws, widths, fold, outs):
+def backward_of(flags_ref, keeps, pointwise, dys, grows, dws, widths, fold, outs):
     found = []
     for keep, turn, dy, grow, dw, width, matrix, (dy_out, dmix_out, dfeat_out) in zip(
-        keeps, turned, dys, grows, dws, widths, (None, fold), outs[0:2]
+        keeps, pointwise, dys, grows, dws, widths, (None, fold), outs[0:2]
     ):
         dy_out[...] = bf(dy)
         dmix, dres = block_backward(keep, turn, dy, grow)
@@ -337,16 +337,12 @@
         grads.append(jnp.concatenate([part, blank], axis=1))
     span = dfeat_a.shape[1]
     nine = jnp.concatenate([air_stack[:, i * wa : i * wa + span] for i in range(3)], axis=0)
-    rest = dot_nt(dfeat_a, jnp.concatenate([nine, jnp.zeros((112, span), BF)], axis=0))
-    dy_a, dy_s = air[5][...], sea[5][...]
-    cells = dy_a.shape[1]
-    zero = lambda rows: jnp.zeros((rows, cells), BF)
-    rest = rest + dot_nt(air[2][...], jnp.concatenate([zero(144), dy_a, zero(96)], axis=0))
-    rest = rest + dot_nt(sea[2][...], jnp.concatenate([zero(160), dy_s, zero(48)], axis=0))
+    parts = [dot_nt(dfeat_a, nine), dot_nt(air[2][...], air[5][...]), dot_nt(sea[2][...], sea[5][...])]
+    rest = jnp.concatenate(parts + [jnp.zeros((64, 256 - sum(x.shape[1] for x in parts)), F32)], axis=1)
     columns = []
     for model, width in ((air, wa), (sea, ws)):
-        feat = model[9][...].astype(F32)
-        columns += depthwise_terms(model[6][...], [rolled(feat, width, by) for by in (-1, 0, 1)], width)
+        dmix = model[6][...]
+        columns += depthwise_terms([rolled(dmix, width, by) for by in (1, 0, -1)], model[9][...].astype(F32), width)
     lanes = iota((64, 256), 1)
     for t, column in enumerate(columns):
         rest = rest + jnp.where(lanes == 208 + t, column, 0.0)
@@ -409,16 +405,14 @@
 
 
 FORMS = {}
+FORM_ROWS = 0
 for _name, _parts, _rows, _columns in (
-    ("aef", 3, 64, 48), ("sef", 3, 64, 192), ("aeb", 3, 48, 64), ("seb", 3, 192, 64),
-    ("aex", 1, 256, 64), ("sex", 1, 256, 64), ("aco_t", 1, 256, 64), ("sco_t", 1, 256, 64),
-    ("aco", 1, 64, 256), ("sco", 1, 64, 256), ("aex_t", 1, 64, 256), ("sex_t", 1, 64, 256),
-    ("ade", 1, 16, 64), ("sde", 1, 48, 64), ("ade_t", 1, 64, 16), ("sde_t", 1, 64, 48),
+    ("aef", 3, 64, 48), ("sef", 3, 64, 192), ("aex", 1, 256, 64), ("sex", 1, 256, 64),
+    ("aco", 1, 64, 256), ("sco", 1, 64, 256), ("ade", 1, 16, 64), ("sde", 1, 48, 64),
     ("adw", 1, 64, 9), ("sdw", 1, 64, 9),
 ):
-    _start = max([start + parts * rows for start, parts, rows, _ in FORMS.values()], default=0)
-    FORMS[_name] = (_start, _parts, _rows, _columns)
-FORM_ROWS = max(start + parts * rows for start, parts, rows, _ in FORMS.values())
+    FORMS[_name] = (FORM_ROWS, _parts, _rows, _columns)
+    FORM_ROWS += _parts * _rows
 
 
 def forms(ref, *names):
@@ -442,29 +436,23 @@
         out[start + rows * part : start + rows * (part + 1), 0:columns] = bf(value)
 
     kinds = aenc.shape[1] // 9
-    for name, weights, padded in (("a", aenc, 16), ("s", senc, 64)):
+    for name, weights, padded in (("aef", aenc, 16), ("sef", senc, 64)):
         column = iota((1, 3 * padded), 1)
         kind = column % padded
-        if name == "a":
+        if name == "aef":
             last = kind == kinds - 1 + SURFACE
             kind = jnp.where(kind < kinds - 1, kind, jnp.where(last, kinds - 1, -(1 << 20)))
         else:
             kind = jnp.where(kind < senc.shape[1] // 9, kind, -(1 << 20))
         for i in range(3):
             wanted = (3 * i + column // padded) * (weights.shape[1] // 9) + kind
-            picked = dot(weights, bf(jnp.where(iota((weights.shape[1], 1), 0) == wanted, 1.0, 0.0)))
-            put(name + "ef", picked, i)
-            put(name + "eb", picked.T, i)
+            put(name, dot(weights, bf(jnp.where(iota((weights.shape[1], 1), 0) == wanted, 1.0, 0.0))), i)
     turn = lambda x: x.astype(F32).T
-    for name, value in (("aex_t", aex_t), ("sex_t", sex_t), ("aco", aco), ("sco", sco), ("sde", sde)):
+    for name, value in (("aco", aco), ("sco", sco), ("sde", sde), ("aex", turn(aex_t)), ("sex", turn(sex_t))):
         put(name, value)
-    for name, value in (("aex", aex_t), ("sex", sex_t), ("aco_t", aco), ("sco_t", sco), ("sde_t", sde)):
-        put(name, turn(value))
-    small = small.astype(F32)
     put("ade", small[0:16])
-    put("ade_t", small[0:16].T)
-    put("adw", small[16:32].T[:, 0:9])
-    put("sdw", small[32:48].T[:, 0:9])
+    put("adw", turn(small[16:32])[:, 0:9])
+    put("sdw", turn(small[32:48])[:, 0:9])
 
 
 def couple_kernel(flags_ref, mine, near, far, at_a, at_b, _, lists_out, cpl_out):
@@ -558,14 +546,13 @@
 def last_kernel(
     flags_ref, a_ref, o_ref, cpl_ref, band_near, band_far, wet_ref, partner_ref,
     acot_ref, ocot_ref, weights_ref,
-    a_out, o_out, air_stack_out, sea_stack_out, air_feat_out, sea_feat_out,
+    air_stack_out, sea_stack_out, air_feat_out, sea_feat_out,
     na, ia, ha, la, ra, ns, is_, hs, ls, rs, pa, ea, ps, es,
     dya, dma, dfa, dys, dms, dfs, near, far,
 ):
     aef, sef, adw, aex, aco, ade, sdw, sex, sco, sde = forms(
         weights_ref, "aef", "sef", "adw", "aex", "aco", "ade", "sdw", "sex", "sco", "sde"
     )
-    aex_t, aco_t, ade_t, sex_t, sco_t, sde_t = forms(weights_ref, "aex_t", "aco_t", "ade_t", "sex_t", "sco_t", "sde_t")
     wa, ws = LANE, wet_ref.shape[1]
     odd = flags_ref[2] > 0
     a, o = a_ref[...], o_ref[...]
@@ -585,13 +572,11 @@
     block_replay(mix(sea_feat, sdw, ws)[0], sea_feat[:, ws:-ws], sex[...], sco[...], keeps[1])
     wet = wet_rows(wet_ref)
     acot = load_rows(acot_ref)
-    turned = ((aex_t[...], aco_t[...], ade_t[...]), (sex_t[...], sco_t[...], sde_t[...]))
+    pointwise = ((aex, aco, ade), (sex, sco, sde))
     backward_of(
-        flags_ref, keeps, turned, (jnp.concatenate([acot, jnp.zeros_like(acot)], axis=0), wet * load_rows(ocot_ref)),
+        flags_ref, keeps, pointwise, (jnp.concatenate([acot, jnp.zeros_like(acot)], axis=0), wet * load_rows(ocot_ref)),
         ((pa, ea), (ps, es)), (adw, sdw), (wa, ws), fold, ((dya, dma, dfa), (dys, dms, dfs), (near, far)),
     )
-    store_rows(a_out, a + dot(ade[...], ra[...])[0:8])
-    store_rows(o_out, o + wet * dot(sde[...], rs[...]))
 
 
 def replay_kernel(
@@ -608,52 +593,53 @@
 
 
 def first_kernel(
-    flags_ref, lists_ref, own, t_near, at_a, at_b, acot_ref, ocot_ref, wet_ref, partner_ref,
+    place, lists_ref, own, t_near, at_a, at_b, acot_ref, ocot_ref, wet_ref, partner_ref,
     na, ia, ha, la, ra, ns, is_, hs, ls, rs, weights_ref,
-    ocot_out, pa, ea, ps, es, dya, dma, dfa, dys, dms, dfs, near, far,
+    air_stack, sea_stack, air_feat, sea_feat, later,
+    ocot_out, dfa, dfs, near, far, grads_out,
+    pa, ea, ps, es, dya, dma, dys, dms,
 ):
-    adw, sdw = forms(weights_ref, "adw", "sdw")
-    aex_t, aco_t, ade_t, sex_t, sco_t, sde_t = forms(weights_ref, "aex_t", "aco_t", "ade_t", "sex_t", "sco_t", "sde_t")
+    adw, aex, aco, ade, sdw, sex, sco, sde = forms(
+        weights_ref, "adw", "aex", "aco", "ade", "sdw", "sex", "sco", "sde"
+    )
     wa, ws = LANE, wet_ref.shape[1]
     fold = fold_matrix(partner_ref)
-    tables = tables_around(flags_ref, own, t_near, at_a, at_b)
+    tables = tables_around(place, own, t_near, at_a, at_b)
     at_air, at_sea = regrid(own_paths(lists_ref, False), tables, False)
     ocot = ocot_ref[...]
     ocot = jnp.where(iota((ocot.shape[0], 1), 0) == 0, ocot + at_sea, ocot)
     ocot_out[...] = ocot
     flux_rows = jnp.concatenate([at_air, jnp.zeros_like(at_air)], axis=0)
-    turned = ((aex_t[...], aco_t[...], ade_t[...]), (sex_t[...], sco_t[...], sde_t[...]))
     backward_of(
-        flags_ref, ((na, ia, ha, la, ra), (ns, is_, hs, ls, rs)), turned,
+        place, ((na, ia, ha, la, ra), (ns, is_, hs, ls, rs)), ((aex, aco, ade), (sex, sco, sde)),
         (jnp.concatenate([acot_ref[...], flux_rows], axis=0), wet_rows(wet_ref) * ocot),
         ((pa, ea), (ps, es)), (adw, sdw), (wa, ws), fold, ((dya, dma, dfa), (dys, dms, dfs), (near, far)),
     )
-
-
-def last_grads_kernel(*refs):
-    air, sea, out, done = refs[0:10], refs[10:20], refs[20], refs[21]
-    done[...] = jnp.zeros_like(done)
-    widths = LANE, (sea[9].shape[1] - sea[0].shape[1]) // 2
-    out[...] = jnp.concatenate(weight_terms(air, sea, widths), axis=1)
-
-
-def first_grads_kernel(*refs):
-    air, sea, later, out, done = refs[0:10], refs[10:20], refs[20], refs[22], refs[23]
-    done[...] = jnp.zeros_like(done)
-    widths = LANE, (sea[9].shape[1] - sea[0].shape[1]) // 2
-    for p, grad in enumerate(weight_terms(air, sea, widths)):
+    air = (na, ha, ra, pa, ea, dya, dma, dfa, air_stack, air_feat)
+    sea = (ns, hs, rs, ps, es, dys, dms, dfs, sea_stack, sea_feat)
+    for p, grad in enumerate(weight_terms(air, sea, (wa, ws))):
         total = bf(later[:, 256 * p : 256 * p + 256] + grad)
         for q in range(4):
             for l in range(2):
                 row = 16 * (16 * q + 2 * p + l)
-                out[row : row + 16, :] = total[16 * q : 16 * q + 16, LANE * l : LANE * (l + 1)]
+                grads_out[row : row + 16, :] = total[16 * q : 16 * q + 16, LANE * l : LANE * (l + 1)]
+
+
+def last_grads_kernel(*refs):
+    air, sea, (a_ref, o_ref, wet_ref, weights_ref), (out, a_out, o_out, done) = refs[0:10], refs[10:20], refs[20:24], refs[24:]
+    done[...] = jnp.zeros_like(done)
+    widths = LANE, wet_ref.shape[1]
+    out[...] = jnp.concatenate(weight_terms(air, sea, widths), axis=1)
+    ade, sde = forms(weights_ref, "ade", "sde")
+    store_rows(a_out, a_ref[...] + dot(ade, air[2][...])[0:8])
+    store_rows(o_out, o_ref[...] + wet_rows(wet_ref) * dot(sde, sea[2][...]))
 
 
 def input_kernel(
     flags_ref, dfa_ref, dfs_ref, from_near, from_far, acot_ref, ocot_ref, partner_ref, weights_ref, *refs,
 ):
     acot_out, ocot_out, table_out = refs[-3:]
-    aeb, seb = forms(weights_ref, "aeb", "seb")
+    aef, sef = forms(weights_ref, "aef", "sef")
     wa, ws = LANE, partner_ref.shape[1]
     fold = fold_matrix(partner_ref)
     up, dn = sides(from_near[...].astype(F32), from_far[...].astype(F32), flags_ref[2] > 0)
@@ -661,8 +647,8 @@
     middle = jnp.zeros((64, dfa.shape[1] - 4 * wa), F32)
     dfa = dfa + jnp.concatenate([dn[:, : 2 * wa], middle, up[:, : 2 * wa]], axis=1)
     dfs = dfs + jnp.concatenate([dn[:, 2 * wa :], up[:, 2 * wa :]], axis=1)
-    dxa = input_cotangent(dfa, aeb, wa, flags_ref, None)
-    dxs = input_cotangent(dfs, seb, ws, flags_ref, fold)
+    dxa = input_cotangent(dfa, aef, wa, flags_ref, None)
+    dxs = input_cotangent(dfs, sef, ws, flags_ref, fold)
     if len(acot_ref.shape) == 3:
         acot_out[...] = load_rows(acot_ref) + dxa[0:8]
         ocot_out[...] = load_rows(ocot_ref) + dxs[0:48]
@@ -848,9 +834,9 @@
         placed_kernel(couple_again_kernel), "couple_again", [head, state, state], (lists, *around(own), a1, o1)
     )
     band_near, band_far = beside(near, far)
-    air_final, sea_final, ast1, sst1, aft1, sft1, *rest = call(
+    ast1, sst1, aft1, sft1, *rest = call(
         placed_kernel(last_kernel), "last",
-        [(air_state.shape, F32), (sea_state.shape, F32), *stacks, *feats, *keeps, *grows, *backs, halo, halo],
+        [*stacks, *feats, *keeps, *grows, *backs, halo, halo],
         (a1, o1, cpl, band_near, band_far, wet_mask, partner, air_cotangent, sea_cotangent,
          weights),
     )
@@ -861,9 +847,10 @@
         keep[5], keep[7], keep[9], ps, es, dys, dms, dfs, sst, sft,
     )
     token = ((8, LANE), F32)
-    later, done = call(
-        last_grads_kernel, "last_grads", [((64, 2048), F32), token],
-        gathered(keep, pa, ea, ps, es, dya, dma, dfa, dys, dms, dfs, ast1, sst1, aft1, sft1), cost=3e9,
+    later, air_final, sea_final, done = call(
+        last_grads_kernel, "last_grads", [((64, 2048), F32), (air_state.shape, F32), (sea_state.shape, F32), token],
+        (*gathered(keep, pa, ea, ps, es, dya, dma, dfa, dys, dms, dfs, ast1, sst1, aft1, sft1),
+         a1, o1, wet_mask, weights), cost=3e9,
     )
     acot, ocot, own = call(
         placed_kernel(input_kernel), "inputs", [((ach, air_sites), F32), ((och, sea_sites), F32), table],
@@ -873,19 +860,18 @@
     keep = call(
         replay_kernel, "replay", keeps, (aft, sft, weights), cost=3e9
     )
-    ocot, pa, ea, ps, es, dya, dma, dfa, dys, dms, dfs, near, far = call(
-        placed_kernel(first_kernel), "first", [((och, sea_sites), F32), *grows, *backs, halo, halo],
-        (lists, *around(own), acot, ocot, wet_mask, partner, *keep, weights),
+    kept = [pltpu.VMEM(shape, kind) for shape, kind in grows + backs[0:2] + backs[3:5]]
+    ocot, dfa, dfs, near, far, grads = call(
+        placed_kernel(first_kernel), "first",
+        [((och, sea_sites), F32), backs[2], backs[5], halo, halo, ((8 * LANE, LANE), BF)],
+        (lists, *around(own), acot, ocot, wet_mask, partner, *keep, weights, ast, sst, aft, sft, later),
+        scratch=kept,
     )
     edge_near, edge_far = beside(near, far)
-    grads, done = call(
-        first_grads_kernel, "first_grads", [((8 * LANE, LANE), BF), token],
-        (*gathered(keep, pa, ea, ps, es, dya, dma, dfa, dys, dms, dfs, ast, sst, aft, sft), later, edge_near), cost=3e9,
-    )
     terms = to_all(grads.reshape(devices, -1, LANE))
     air_grad, ocot, own = call(
         placed_kernel(input_kernel), "first_inputs", [(air_state.shape, F32), ((och, sea_sites), F32), table],
-        (dfa, dfs, edge_near, edge_far, acot, ocot, partner, weights, done), cost=5e10,
+        (dfa, dfs, edge_near, edge_far, acot, ocot, partner, weights), cost=5e10,
     )
     tables = around(own)
     (sums,) = call(total_kernel, "total", [(terms.shape, BF)], (terms, tables[2]))

time: 111 us -> 110 us (level)
  local copies, waits for them, and re-layouts: 3.01 us -> 1.15 us
  waiting for transfers between devices: 18.4 us -> 19.8 us
    unnamed x29 -> x25, local copies, waits for them, and re-layouts: 2.98 us -> 1.13 us
    all_to_all x2, waiting for transfers between devices: 11.1 us -> 12.5 us  [to_all(): return lax.all_to_all(blocks, 'tile', 0, 0)]
    ppermute x3, starting transfers between devices: 14.5 us -> 13.3 us  [around(): near = lax.ppermute(table, 'tile', [(i, i ^ 1) for i in range(length)])]
    pallas_call x15 -> x14, Pallas kernels: 31.2 us -> 31.2 us  [call(): pl.pallas_call(kernel, out_shape=[jax.ShapeDtypeStruct(shape, kind) for s...]
  transfers between devices with their start and end apart: 23 -> 23, of which waited for: 11 -> 10; matrix products, arithmetic and copies ran while one was open for 1% -> 1% of each run, Pallas kernels for 12% -> 10%
where the time goes in v2:
time: 110 us
  starting transfers between devices  55.3 us (50%)
  Pallas kernels  31.2 us (28%)
  waiting for transfers between devices  19.8 us (18%)
  other arithmetic  1.33 us (1%)
  local copies, waits for them, and re-layouts  1.15 us (1%)
    pallas_call x14, Pallas kernels, call(): pl.pallas_call(kernel, out_shape=[jax.ShapeDtypeStruct(shape, kind) for s...  31.2 us
    all_to_all x2, starting transfers between devices, to_all(): return lax.all_to_all(blocks, 'tile', 0, 0)  14 us
    ppermute x3, starting transfers between devices, around(): near = lax.ppermute(table, 'tile', [(i, i ^ 1) for i in range(length)])  13.3 us
    all_to_all x2, waiting for transfers between devices, to_all(): return lax.all_to_all(blocks, 'tile', 0, 0)  12.5 us
    ppermute x4, starting transfers between devices, chips_beside(): return (lax.ppermute(at_a, 'tile', first), at_b)  11.3 us
    ppermute x5, starting transfers between devices, beside(): return (lax.ppermute(near, 'tile', chip), far)  10.6 us
    ppermute x4, waiting for transfers between devices, chips_beside(): return (lax.ppermute(at_a, 'tile', first), at_b)  3.51 us
    ppermute x5, starting transfers between devices, beside(): far = lax.ppermute(far, 'tile', other)  3.48 us
  transfers between devices with their start and end apart: 23, of which 10 were waited for; matrix products, arithmetic and copies ran while one was open for 1% of the time, Pallas kernels for 10%

profile of v2, /device:TPU:0, one launch (start us, length us, event | category | flops | bytes accessed | tf_op | source)
XLA Modules:
  0.0 109.7 jit_solution(3853822858448861628)
XLA Ops:
  0.6 2.1 %pack.1 = (f32[56,1024]{1,0:T(8,128)}, bf16[80,1024]{1,0:T(8,128)(2,1)}, bf16[80,1024]{1,0:T(8,128)(2,1)}, bf16[16,1024]{1,0:T(8,128)(2,1)}, bf16[16,1024]{1,0:T(8,128)(2,1)}) custom-call(s32[1,5]{1,0:T(1,128)} %refs_0_.3, f32[8,8,128]{2,1,0:T(8,128)} %refs_0_.5, f32[48,2,512]{2,1,0:T(2,128)} %refs_1_.6, f32[4,8,128]{2,1,0:T(8,128)} %refs_3_.1, ...), custom_call_target="tpu_custom_call" | custom-call | tf_op jit(solution)/shard_map/pack/pallas_call | solution.py:724
  4.0 3.8 %collective-permute-start.2 = (bf16[16,1024]{1,0:T(8,128)(2,1)}, bf16[16,1024]{1,0:T(8,128)(2,1)S(1)}, u32[]{:S(2)}, u32[]{:S(2)}) collective-permute-start(bf16[16,1024]{1,0:T(8,128)(2,1)} %get-tuple-element.95), channel_id=1, source_target_pairs={{0,2},{1,3},{2,0},{3,1},{4,6},{5,7},{6,4},{7,5},{8,10},{9,11},{10,... | collective-permute-start | bytes 98312 | tf_op jit(solution)/shard_map/ppermute | solution.py:741
  8.4 1.3 %fusion.5.refs_7_ = bf16[48,64]{1,0:T(8,128)(2,1)} fusion(bf16[9,64]{1,0:T(8,128)(2,1)} %bitcast.23, bf16[9,64]{1,0:T(8,128)(2,1)} %bitcast.24, bf16[12,64]{1,0:T(8,128)(2,1)} %param.40), kind=kLoop, calls=%fused_computation.15 | loop fusion | flops 43008 | bytes 9984 | tf_op jit(solution)/shard_map/concatenate | solution.py:805
  9.8 2.2 %prepare.1.refs_5_.refs_9_.refs_23_.refs_7_.weights_ref.refs_19_ = bf16[1216,256]{1,0:T(8,128)(2,1)} custom-call(bf16[64,81]{1,0:T(8,128)(2,1)} %refs_0_.4, bf16[64,468]{1,0:T(8,128)(2,1)} %refs_1_.5, bf16[64,256]{1,0:T(8,128)(2,1)} %bitcast.27, bf16[64,256]{1,0:T(8,128)(2,1)} %bitcast.28, bf16[64,256]{1,0:T(8,128)(2,1)} %refs_4_.2, ...), custom_call_target="tpu_custom_call" | custom-call | flops 3000000000 | bytes 4194304 | tf_op jit(solution)/shard_map/prepare/pallas_call | solution.py:724
  12.8 1.1 copy-done
  13.9 1.4 %couple.1 = (bf16[80,1024]{1,0:T(8,128)(2,1)S(1)}, bf16[16,1024]{1,0:T(8,128)(2,1)S(1)}) custom-call(f32[56,1024]{1,0:T(8,128)S(1)} %copy-done.4, bf16[80,1024]{1,0:T(8,128)(2,1)S(1)} %collective-permute-done.refs_1_.refs_3_, bf16[80,1024]{1,0:T(8,128)(2,1)S(1)} %collective-permute-done.1.refs_2_.refs_4_, ...), custom_call_target="tpu_custom_call" | custom-call | tf_op jit(solution)/shard_map/couple/pallas_call | solution.py:724
  16.9 2.6 %forward.1 = (f32[8,1024]{1,0:T(8,128)S(1)}, f32[48,1024]{1,0:T(8,128)S(1)}, bf16[48,128]{1,0:T(8,128)(2,1)S(1)}, bf16[48,1536]{1,0:T(8,128)(2,1)S(1)}, bf16[192...) custom-call(f32[8,8,128]{2,1,0:T(8,128)S(1)} %copy-done.6, ...), custom_call_target="tpu_custom_call" | custom-call | tf_op jit(solution)/shard_map/forward/pallas_call | solution.py:724
  19.5 6.6 %collective-permute-start.6 = (bf16[48,128]{1,0:T(8,128)(2,1)S(1)}, bf16[48,128]{1,0:T(8,128)(2,1)S(1)}, u32[]{:S(2)}, u32[]{:S(2)}) collective-permute-start(bf16[48,128]{1,0:T(8,128)(2,1)S(1)} %get-tuple-element.101.refs_1_), channel_id=1, source_target_pairs={{0,1},{1,0},{2,3},{3,2},{4,5},{5,4},{6,7},{7,6},{8,9},{9,8},{10,11... | collective-permute-start | bytes 36872 | tf_op jit(solution)/shard_map/ppermute | solution.py:758
  27.0 2.9 %collective-permute-start.7 = (bf16[96,128]{1,0:T(8,128)(2,1)S(1)}, bf16[96,128]{1,0:T(8,128)(2,1)S(1)}, u32[]{:S(2)}, u32[]{:S(2)}) collective-permute-start(bf16[96,128]{1,0:T(8,128)(2,1)S(1)} %constant_dynamic-update-slice_fusion), channel_id=1, source_target_pairs={{0,2},{1,3},{2,0},{3,1},{4,6},{5,7},{6,4},{7,5},{8,10},{9,11},{10,... | collective-permute-start | bytes 73736 | tf_op jit(solution)/shard_map/ppermute | solution.py:741
  30.6 1.1 %collective-permute-done.7.refs_3_ = bf16[96,128]{1,0:T(8,128)(2,1)S(1)} collective-permute-done((bf16[96,128]{1,0:T(8,128)(2,1)S(1)}, bf16[96,128]{1,0:T(8,128)(2,1)S(1)}, u32[]{:S(2)}, u32[]{:S(2)}) %collective-permute-start.7) | collective-permute-done | bytes 24608 | tf_op jit(solution)/shard_map/ppermute | solution.py:741
  31.7 1.3 %couple_again.1 = (bf16[16,1024]{1,0:T(8,128)(2,1)S(1)}, bf16[64,1024]{1,0:T(8,128)(2,1)S(1)}, bf16[64,1024]{1,0:T(8,128)(2,1)S(1)}) custom-call(bf16[80,1024]{1,0:T(8,128)(2,1)S(1)} %get-tuple-element.100.refs_0_, bf16[48,128]{1,0:T(8,128)(2,1)S(1)} %get-tuple-element.101.refs_1_, bf16[48,128]{1,0:T(8,128)(2,1)S(1)} %collective-permute-done.6.refs_2_, ...), custom_call_target="tpu_custom_call" | custom-call | tf_op jit(solution)/shard_map/couple_again/pallas_call | solution.py:724
  33.7 7.7 %collective-permute-start.9 = (bf16[64,1024]{1,0:T(8,128)(2,1)S(1)}, bf16[64,1024]{1,0:T(8,128)(2,1)S(1)}, u32[]{:S(2)}, u32[]{:S(2)}) collective-permute-start(bf16[64,1024]{1,0:T(8,128)(2,1)S(1)} %get-tuple-element.103), channel_id=1, source_target_pairs={{0,1},{1,0},{2,3},{3,2},{4,5},{5,4},{6,7},{7,6},{8,9},{9,8},{10,11... | collective-permute-start | bytes 393224 | tf_op jit(solution)/shard_map/ppermute | solution.py:749
  41.4 1.0 collective-permute-done.9.refs_3_
  42.4 5.1 %last.1 = (bf16[48,1536]{1,0:T(8,128)(2,1)S(1)}, bf16[192,3072]{1,0:T(8,128)(2,1)S(1)}, bf16[64,1280]{1,0:T(8,128)(2,1)S(1)}, bf16[64,2048]{1,0:T(8,128)(2,1)S(1...) custom-call(f32[8,1024]{1,0:T(8,128)S(1)} %get-tuple-element.98.refs, ...), custom_call_target="tpu_custom_call" | custom-call | tf_op jit(solution)/shard_map/last/pallas_call | solution.py:724
  47.4 1.6 %collective-permute-start.11 = (bf16[64,1280]{1,0:T(8,128)(2,1)S(1)}, bf16[64,1280]{1,0:T(8,128)(2,1)S(1)}, u32[]{:S(2)}, u32[]{:S(2)}) collective-permute-start(bf16[64,1280]{1,0:T(8,128)(2,1)S(1)} %get-tuple-element.127), channel_id=1, source_target_pairs={{0,1},{1,0},{2,3},{3,2},{4,5},{5,4},{6,7},{7,6},{8,9},{9,8},{10,11... | collective-permute-start | bytes 491528 | tf_op jit(solution)/shard_map/ppermute | solution.py:749
  49.1 0.8 collective-permute-start.12
  49.9 2.7 %last_grads.1 = (f32[64,2048]{1,0:T(8,128)S(1)}, f32[8,8,128]{2,1,0:T(8,128)}, f32[48,2,512]{2,1,0:T(2,128)}, f32[8,128]{1,0:T(8,128)S(1)}) custom-call(f32[64,1024]{1,0:T(8,128)S(1)} %get-tuple-element.105.refs_0_, bf16[256,1024]{1,0:T(8,128)(2,1)S(1)} %get-tuple-element.106.refs_1_, bf16[64,1024]{1,0:T(8,128)(2,1)S(1)} %get-tuple-element.107.refs_2_, ...), custom_call_target="tpu_custom_call" | custom-call | flops 3000000000 | bytes 4194304 | tf_op jit(solution)/shard_map/last_grads/pallas_call | solution.py:724
  52.6 0.9 inputs.1
  53.6 6.5 %collective-permute-start.13 = (bf16[48,128]{1,0:T(8,128)(2,1)S(1)}, bf16[48,128]{1,0:T(8,128)(2,1)S(1)}, u32[]{:S(2)}, u32[]{:S(2)}) collective-permute-start(bf16[48,128]{1,0:T(8,128)(2,1)S(1)} %get-tuple-element.130.refs_1_), channel_id=1, source_target_pairs={{0,1},{1,0},{2,3},{3,2},{4,5},{5,4},{6,7},{7,6},{8,9},{9,8},{10,11... | collective-permute-start | bytes 36872 | tf_op jit(solution)/shard_map/ppermute | solution.py:758
  60.9 2.8 %collective-permute-start.14 = (bf16[96,128]{1,0:T(8,128)(2,1)S(1)}, bf16[96,128]{1,0:T(8,128)(2,1)S(1)}, u32[]{:S(2)}, u32[]{:S(2)}) collective-permute-start(bf16[96,128]{1,0:T(8,128)(2,1)S(1)} %constant_dynamic-update-slice_fusion.2), channel_id=1, source_target_pairs={{0,2},{1,3},{2,0},{3,1},{4,6},{5,7},{6,4},{7,5},{8,10},{9,11},{10,... | collective-permute-start | bytes 73736 | tf_op jit(solution)/shard_map/ppermute | solution.py:741
  64.3 2.3 %replay.1 = (f32[64,1024]{1,0:T(8,128)S(1)}, f32[8,1024]{1,0:T(8,128)S(1)}, bf16[256,1024]{1,0:T(8,128)(2,1)S(1)}, bf16[256,1024]{1,0:T(8,128)(2,1)S(1)}, bf16[6...) custom-call(bf16[64,1280]{1,0:T(8,128)(2,1)S(1)} %get-tuple-element., ...), custom_call_target="tpu_custom_call" | custom-call | flops 3000000000 | bytes 4194304 | tf_op jit(solution)/shard_map/replay/pallas_call | solution.py:724
  66.6 5.4 %first.1 = (f32[48,1024]{1,0:T(8,128)S(1)}, f32[64,1280]{1,0:T(8,128)S(1)}, f32[64,2048]{1,0:T(8,128)S(1)}, bf16[64,1280]{1,0:T(8,128)(2,1)S(1)}, bf16[64,1280]{...) custom-call(bf16[80,1024]{1,0:T(8,128)(2,1)S(1)} %get-tuple-element.100.refs_0_, ...), custom_call_target="tpu_custom_call" | custom-call | tf_op jit(solution)/shard_map/first/pallas_call | solution.py:724
  72.8 11.4 %all-to-all-start = ((bf16[32,32,128]{2,1,0:T(8,128)(2,1)}), bf16[32,32,128]{2,1,0:T(8,128)(2,1)S(1)}, u32[]{:S(2)}, u32[]{:S(2)}) async-start(bf16[32,32,128]{2,1,0:T(8,128)(2,1)} %bitcast.9), calls=%async_computation | async-start | bytes 524288 | tf_op jit(solution)/shard_map/all_to_all | solution.py:753
  84.2 1.4 %first_inputs.1 = (f32[8,8,128]{2,1,0:T(8,128)}, f32[48,1024]{1,0:T(8,128)S(1)}, bf16[48,128]{1,0:T(8,128)(2,1)S(1)}) custom-call(f32[64,1280]{1,0:T(8,128)S(1)} %get-tuple-element.148.refs_0_, f32[64,2048]{1,0:T(8,128)S(1)} %get-tuple-element.149.refs_1_, bf16[64,1280]{1,0:T(8,128)(2,1)S(1)} %collective-permute-done.16.refs_2_, ...), custom_call_target="tpu_custom_call" | custom-call | flops 49999998976 | bytes 4194304 | tf_op jit(solution)/shard_map/first_inputs/pallas_call | solution.py:724
  85.9 0.9 collective-permute-done.18.refs_2_
  86.8 1.8 %collective-permute-start.19 = (bf16[96,128]{1,0:T(8,128)(2,1)S(1)}, bf16[96,128]{1,0:T(8,128)(2,1)S(1)}, u32[]{:S(2)}, u32[]{:S(2)}) collective-permute-start(bf16[96,128]{1,0:T(8,128)(2,1)S(1)} %constant_dynamic-update-slice_fusion.4), channel_id=1, source_target_pairs={{0,2},{1,3},{2,0},{3,1},{4,6},{5,7},{6,4},{7,5},{8,10},{9,11},{10,... | collective-permute-start | bytes 73736 | tf_op jit(solution)/shard_map/ppermute | solution.py:741
  89.2 1.6 %collective-permute-done.19.refs_3_._ = bf16[96,128]{1,0:T(8,128)(2,1)S(1)} collective-permute-done((bf16[96,128]{1,0:T(8,128)(2,1)S(1)}, bf16[96,128]{1,0:T(8,128)(2,1)S(1)}, u32[]{:S(2)}, u32[]{:S(2)}) %collective-permute-start.19) | collective-permute-done | bytes 24608 | tf_op jit(solution)/shard_map/ppermute | solution.py:741
  90.8 4.0 %all-to-all-done.terms_ref = bf16[32,32,128]{2,1,0:T(8,128)(2,1)S(1)} async-done(((bf16[32,32,128]{2,1,0:T(8,128)(2,1)}), bf16[32,32,128]{2,1,0:T(8,128)(2,1)S(1)}, u32[]{:S(2)}, u32[]{:S(2)}) %all-to-all-start) | async-done | bytes 262176 | tf_op jit(solution)/shard_map/all_to_all | solution.py:753
  95.5 2.6 %all-to-all-start.1 = ((bf16[32,32,128]{2,1,0:T(8,128)(2,1)}), bf16[32,32,128]{2,1,0:T(8,128)(2,1)S(1)}, u32[]{:S(2)}, u32[]{:S(2)}) async-start(bf16[32,32,128]{2,1,0:T(8,128)(2,1)} %total.1), calls=%async_computation.1 | async-start | bytes 524288 | tf_op jit(solution)/shard_map/all_to_all | solution.py:753
  98.2 2.0 %final.1 = (f32[48,2,512]{2,1,0:T(2,128)}, f32[4,8,128]{2,1,0:T(8,128)}) custom-call(bf16[80,1024]{1,0:T(8,128)(2,1)S(1)} %get-tuple-element.100.refs_0_, bf16[48,128]{1,0:T(8,128)(2,1)S(1)} %get-tuple-element.154.refs_1_, bf16[48,128]{1,0:T(8,128)(2,1)S(1)} %collective-permute-done.18.refs_2_, bf16[96,128]{1,0:T(8,128)(2,1)S(1)} %collective-permute-done.19.refs_3_._, ...), custom_call_target="tpu_custom_call" | custom-call | flops 49999998976 | bytes 4194304 | tf_op jit(solution)/shard_map/final/pallas_call | solution.py:724
  100.2 8.5 %all-to-all-done.1.refs_0_ = bf16[32,32,128]{2,1,0:T(8,128)(2,1)S(1)} async-done(((bf16[32,32,128]{2,1,0:T(8,128)(2,1)}), bf16[32,32,128]{2,1,0:T(8,128)(2,1)S(1)}, u32[]{:S(2)}, u32[]{:S(2)}) %all-to-all-start.1) | async-done | bytes 262176 | tf_op jit(solution)/shard_map/all_to_all | solution.py:753
  108.7 1.0 unpack.1
  (57 shorter events, 10.4 us)
Async XLA Ops:
  2.8 10.0 %collective-permute-start = (bf16[80,1024]{1,0:T(8,128)(2,1)}, bf16[80,1024]{1,0:T(8,128)(2,1)S(1)}, u32[]{:S(2)}, u32[]{:S(2)}) collective-permute-start(bf16[80,1024]{1,0:T(8,128)(2,1)} %get-tuple-element.93), channel_id=1, source_target_pairs={{0,1},{1,0},{2,3},{3,2},{4,5},{5,4},{6,7},{7,6},{8,9},{9,8},{10,11... | collective-permute-start | bytes 491528 | tf_op jit(solution)/shard_map/ppermute | solution.py:749
  3.3 9.5 %collective-permute-start.1 = (bf16[80,1024]{1,0:T(8,128)(2,1)}, bf16[80,1024]{1,0:T(8,128)(2,1)S(1)}, u32[]{:S(2)}, u32[]{:S(2)}) collective-permute-start(bf16[80,1024]{1,0:T(8,128)(2,1)} %get-tuple-element.94), channel_id=1, source_target_pairs={{1,2},{2,1},{3,4},{4,3},{5,6},{6,5},{7,8},{8,7},{9,10},{10,9},{11,... | collective-permute-start | bytes 491528 | tf_op jit(solution)/shard_map/ppermute | solution.py:748
  4.0 8.8 %collective-permute-start.2 = (bf16[16,1024]{1,0:T(8,128)(2,1)}, bf16[16,1024]{1,0:T(8,128)(2,1)S(1)}, u32[]{:S(2)}, u32[]{:S(2)}) collective-permute-start(bf16[16,1024]{1,0:T(8,128)(2,1)} %get-tuple-element.95), channel_id=1, source_target_pairs={{0,2},{1,3},{2,0},{3,1},{4,6},{5,7},{6,4},{7,5},{8,10},{9,11},{10,... | collective-permute-start | bytes 98312 | tf_op jit(solution)/shard_map/ppermute | solution.py:741
  7.8 5.0 %collective-permute-start.3 = (bf16[16,1024]{1,0:T(8,128)(2,1)}, bf16[16,1024]{1,0:T(8,128)(2,1)S(1)}, u32[]{:S(2)}, u32[]{:S(2)}) collective-permute-start(bf16[16,1024]{1,0:T(8,128)(2,1)} %get-tuple-element.96), channel_id=1, source_target_pairs={{2,4},{3,5},{4,2},{5,3},{6,8},{7,9},{8,6},{9,7},{10,12},{11,13},{1... | collective-permute-start | bytes 98312 | tf_op jit(solution)/shard_map/ppermute | solution.py:740
  9.8 7.1 %copy-start.2 = (f32[48,2,512]{2,1,0:T(2,128)S(1)}, f32[48,2,512]{2,1,0:T(2,128)}, u32[]{:S(2)}) copy-start(f32[48,2,512]{2,1,0:T(2,128)} %refs_1_.6) | copy-start | bytes 589828
  9.8 7.1 %copy-start.6 = (f32[8,8,128]{2,1,0:T(8,128)S(1)}, f32[8,8,128]{2,1,0:T(8,128)}, u32[]{:S(2)}) copy-start(f32[8,8,128]{2,1,0:T(8,128)} %refs_0_.5) | copy-start | bytes 98308
  9.8 7.1 %copy-start.7 = (s32[2,512]{1,0:T(2,128)S(1)}, s32[2,512]{1,0:T(2,128)}, u32[]{:S(2)}) copy-start(s32[2,512]{1,0:T(2,128)} %refs_7_.5) | copy-start | bytes 12292
  9.8 7.1 %copy-start.8 = (s32[512]{0:T(512)S(1)}, s32[512]{0:T(512)}, u32[]{:S(2)}) copy-start(s32[512]{0:T(512)} %param.32) | copy-start | bytes 6148
  15.2 27.1 %copy-start.1 = (bf16[1216,256]{1,0:T(8,128)(2,1)S(1)}, bf16[1216,256]{1,0:T(8,128)(2,1)}, u32[]{:S(2)}) copy-start(bf16[1216,256]{1,0:T(8,128)(2,1)} %prepare.1.refs_5_.refs_9_.refs_23_.refs_7_.weights_ref.refs_19_) | copy-start | bytes 1867780
  15.2 27.1 %copy-start.3 = (f32[48,2,512]{2,1,0:T(2,128)S(1)}, f32[48,2,512]{2,1,0:T(2,128)}, u32[]{:S(2)}) copy-start(f32[48,2,512]{2,1,0:T(2,128)} %refs_5_.5) | copy-start | bytes 589828
  15.2 27.1 %copy-start.5 = (f32[8,8,128]{2,1,0:T(8,128)S(1)}, f32[8,8,128]{2,1,0:T(8,128)}, u32[]{:S(2)}) copy-start(f32[8,8,128]{2,1,0:T(8,128)} %refs_4_.3) | copy-start | bytes 98308
  15.3 1.6 %collective-permute-start.4 = (bf16[16,1024]{1,0:T(8,128)(2,1)S(1)}, bf16[16,1024]{1,0:T(8,128)(2,1)S(1)}, u32[]{:S(2)}, u32[]{:S(2)}) collective-permute-start(bf16[16,1024]{1,0:T(8,128)(2,1)S(1)} %get-tuple-element.97.refs_2_), channel_id=1, source_target_pairs={{0,1},{1,0},{2,3},{3,2},{4,5},{5,4},{6,7},{7,6},{8,9},{9,8},{10,11... | collective-permute-start | bytes 98312 | tf_op jit(solution)/shard_map/ppermute | solution.py:749
  16.0 0.9 collective-permute-start.5
  19.5 7.4 %collective-permute-start.6 = (bf16[48,128]{1,0:T(8,128)(2,1)S(1)}, bf16[48,128]{1,0:T(8,128)(2,1)S(1)}, u32[]{:S(2)}, u32[]{:S(2)}) collective-permute-start(bf16[48,128]{1,0:T(8,128)(2,1)S(1)} %get-tuple-element.101.refs_1_), channel_id=1, source_target_pairs={{0,1},{1,0},{2,3},{3,2},{4,5},{5,4},{6,7},{7,6},{8,9},{9,8},{10,11... | collective-permute-start | bytes 36872 | tf_op jit(solution)/shard_map/ppermute | solution.py:758
  27.0 4.7 %collective-permute-start.7 = (bf16[96,128]{1,0:T(8,128)(2,1)S(1)}, bf16[96,128]{1,0:T(8,128)(2,1)S(1)}, u32[]{:S(2)}, u32[]{:S(2)}) collective-permute-start(bf16[96,128]{1,0:T(8,128)(2,1)S(1)} %constant_dynamic-update-slice_fusion), channel_id=1, source_target_pairs={{0,2},{1,3},{2,0},{3,1},{4,6},{5,7},{6,4},{7,5},{8,10},{9,11},{10,... | collective-permute-start | bytes 73736 | tf_op jit(solution)/shard_map/ppermute | solution.py:741
  29.9 1.8 %collective-permute-start.8 = (bf16[96,128]{1,0:T(8,128)(2,1)S(1)}, bf16[96,128]{1,0:T(8,128)(2,1)S(1)}, u32[]{:S(2)}, u32[]{:S(2)}) collective-permute-start(bf16[96,128]{1,0:T(8,128)(2,1)S(1)} %constant_dynamic-update-slice_fusion), channel_id=1, source_target_pairs={{2,4},{3,5},{4,2},{5,3},{6,8},{7,9},{8,6},{9,7},{10,12},{11,13},{1... | collective-permute-start | bytes 73736 | tf_op jit(solution)/shard_map/ppermute | solution.py:740
  33.0 8.3 %collective-permute-start.10 = (bf16[64,1024]{1,0:T(8,128)(2,1)S(1)}, bf16[64,1024]{1,0:T(8,128)(2,1)S(1)}, u32[]{:S(2)}, u32[]{:S(2)}) collective-permute-start(bf16[64,1024]{1,0:T(8,128)(2,1)S(1)} %get-tuple-element.104), channel_id=1, source_target_pairs={{1,2},{2,1},{3,4},{4,3},{5,6},{6,5},{7,8},{8,7},{9,10},{10,9},{11,... | collective-permute-start | bytes 393224 | tf_op jit(solution)/shard_map/ppermute | solution.py:748
  33.7 8.6 %collective-permute-start.9 = (bf16[64,1024]{1,0:T(8,128)(2,1)S(1)}, bf16[64,1024]{1,0:T(8,128)(2,1)S(1)}, u32[]{:S(2)}, u32[]{:S(2)}) collective-permute-start(bf16[64,1024]{1,0:T(8,128)(2,1)S(1)} %get-tuple-element.103), channel_id=1, source_target_pairs={{0,1},{1,0},{2,3},{3,2},{4,5},{5,4},{6,7},{7,6},{8,9},{9,8},{10,11... | collective-permute-start | bytes 393224 | tf_op jit(solution)/shard_map/ppermute | solution.py:749
  47.4 5.2 %collective-permute-start.11 = (bf16[64,1280]{1,0:T(8,128)(2,1)S(1)}, bf16[64,1280]{1,0:T(8,128)(2,1)S(1)}, u32[]{:S(2)}, u32[]{:S(2)}) collective-permute-start(bf16[64,1280]{1,0:T(8,128)(2,1)S(1)} %get-tuple-element.127), channel_id=1, source_target_pairs={{0,1},{1,0},{2,3},{3,2},{4,5},{5,4},{6,7},{7,6},{8,9},{9,8},{10,11... | collective-permute-start | bytes 491528 | tf_op jit(solution)/shard_map/ppermute | solution.py:749
  49.1 3.5 %collective-permute-start.12 = (bf16[64,1280]{1,0:T(8,128)(2,1)S(1)}, bf16[64,1280]{1,0:T(8,128)(2,1)S(1)}, u32[]{:S(2)}, u32[]{:S(2)}) collective-permute-start(bf16[64,1280]{1,0:T(8,128)(2,1)S(1)} %get-tuple-element.128), channel_id=1, source_target_pairs={{1,2},{2,1},{3,4},{4,3},{5,6},{6,5},{7,8},{8,7},{9,10},{10,9},{11,... | collective-permute-start | bytes 491528 | tf_op jit(solution)/shard_map/ppermute | solution.py:748
  53.6 7.3 %collective-permute-start.13 = (bf16[48,128]{1,0:T(8,128)(2,1)S(1)}, bf16[48,128]{1,0:T(8,128)(2,1)S(1)}, u32[]{:S(2)}, u32[]{:S(2)}) collective-permute-start(bf16[48,128]{1,0:T(8,128)(2,1)S(1)} %get-tuple-element.130.refs_1_), channel_id=1, source_target_pairs={{0,1},{1,0},{2,3},{3,2},{4,5},{5,4},{6,7},{7,6},{8,9},{9,8},{10,11... | collective-permute-start | bytes 36872 | tf_op jit(solution)/shard_map/ppermute | solution.py:758
  60.9 5.7 %collective-permute-start.14 = (bf16[96,128]{1,0:T(8,128)(2,1)S(1)}, bf16[96,128]{1,0:T(8,128)(2,1)S(1)}, u32[]{:S(2)}, u32[]{:S(2)}) collective-permute-start(bf16[96,128]{1,0:T(8,128)(2,1)S(1)} %constant_dynamic-update-slice_fusion.2), channel_id=1, source_target_pairs={{0,2},{1,3},{2,0},{3,1},{4,6},{5,7},{6,4},{7,5},{8,10},{9,11},{10,... | collective-permute-start | bytes 73736 | tf_op jit(solution)/shard_map/ppermute | solution.py:741
  63.6 3.0 %collective-permute-start.15 = (bf16[96,128]{1,0:T(8,128)(2,1)S(1)}, bf16[96,128]{1,0:T(8,128)(2,1)S(1)}, u32[]{:S(2)}, u32[]{:S(2)}) collective-permute-start(bf16[96,128]{1,0:T(8,128)(2,1)S(1)} %constant_dynamic-update-slice_fusion.2), channel_id=1, source_target_pairs={{2,4},{3,5},{4,2},{5,3},{6,8},{7,9},{8,6},{9,7},{10,12},{11,13},{1... | collective-permute-start | bytes 73736 | tf_op jit(solution)/shard_map/ppermute | solution.py:740
  72.1 12.1 %collective-permute-start.16 = (bf16[64,1280]{1,0:T(8,128)(2,1)S(1)}, bf16[64,1280]{1,0:T(8,128)(2,1)S(1)}, u32[]{:S(2)}, u32[]{:S(2)}) collective-permute-start(bf16[64,1280]{1,0:T(8,128)(2,1)S(1)} %get-tuple-element.150), channel_id=1, source_target_pairs={{0,1},{1,0},{2,3},{3,2},{4,5},{5,4},{6,7},{7,6},{8,9},{9,8},{10,11... | collective-permute-start | bytes 491528 | tf_op jit(solution)/shard_map/ppermute | solution.py:749
  72.1 12.1 %collective-permute-start.17 = (bf16[64,1280]{1,0:T(8,128)(2,1)S(1)}, bf16[64,1280]{1,0:T(8,128)(2,1)S(1)}, u32[]{:S(2)}, u32[]{:S(2)}) collective-permute-start(bf16[64,1280]{1,0:T(8,128)(2,1)S(1)} %get-tuple-element.151), channel_id=1, source_target_pairs={{1,2},{2,1},{3,4},{4,3},{5,6},{6,5},{7,8},{8,7},{9,10},{10,9},{11,... | collective-permute-start | bytes 491528 | tf_op jit(solution)/shard_map/ppermute | solution.py:748
  72.8 22.0 %all-to-all-start = ((bf16[32,32,128]{2,1,0:T(8,128)(2,1)}), bf16[32,32,128]{2,1,0:T(8,128)(2,1)S(1)}, u32[]{:S(2)}, u32[]{:S(2)}) async-start(bf16[32,32,128]{2,1,0:T(8,128)(2,1)} %bitcast.9), calls=%async_computation | async-start | bytes 524288 | tf_op jit(solution)/shard_map/all_to_all | solution.py:753
  85.6 1.2 %collective-permute-start.18 = (bf16[48,128]{1,0:T(8,128)(2,1)S(1)}, bf16[48,128]{1,0:T(8,128)(2,1)S(1)}, u32[]{:S(2)}, u32[]{:S(2)}) collective-permute-start(bf16[48,128]{1,0:T(8,128)(2,1)S(1)} %get-tuple-element.154.refs_1_), channel_id=1, source_target_pairs={{0,1},{1,0},{2,3},{3,2},{4,5},{5,4},{6,7},{7,6},{8,9},{9,8},{10,11... | collective-permute-start | bytes 36872 | tf_op jit(solution)/shard_map/ppermute | solution.py:758
  86.8 4.0 %collective-permute-start.19 = (bf16[96,128]{1,0:T(8,128)(2,1)S(1)}, bf16[96,128]{1,0:T(8,128)(2,1)S(1)}, u32[]{:S(2)}, u32[]{:S(2)}) collective-permute-start(bf16[96,128]{1,0:T(8,128)(2,1)S(1)} %constant_dynamic-update-slice_fusion.4), channel_id=1, source_target_pairs={{0,2},{1,3},{2,0},{3,1},{4,6},{5,7},{6,4},{7,5},{8,10},{9,11},{10,... | collective-permute-start | bytes 73736 | tf_op jit(solution)/shard_map/ppermute | solution.py:741
  88.6 9.6 %collective-permute-start.20 = (bf16[96,128]{1,0:T(8,128)(2,1)S(1)}, bf16[96,128]{1,0:T(8,128)(2,1)S(1)}, u32[]{:S(2)}, u32[]{:S(2)}) collective-permute-start(bf16[96,128]{1,0:T(8,128)(2,1)S(1)} %constant_dynamic-update-slice_fusion.4), channel_id=1, source_target_pairs={{2,4},{3,5},{4,2},{5,3},{6,8},{7,9},{8,6},{9,7},{10,12},{11,13},{1... | collective-permute-start | bytes 73736 | tf_op jit(solution)/shard_map/ppermute | solution.py:740
  95.5 13.2 %all-to-all-start.1 = ((bf16[32,32,128]{2,1,0:T(8,128)(2,1)}), bf16[32,32,128]{2,1,0:T(8,128)(2,1)S(1)}, u32[]{:S(2)}, u32[]{:S(2)}) async-start(bf16[32,32,128]{2,1,0:T(8,128)(2,1)} %total.1), calls=%async_computation.1 | async-start | bytes 524288 | tf_op jit(solution)/shard_map/all_to_all | solution.py:753
  98.1 10.6 %copy-start.9 = (s32[1,468]{1,0:T(1,128)S(1)}, s32[1,468]{1,0:T(1,128)}, u32[]{:S(2)}) copy-start(s32[1,468]{1,0:T(1,128)} %constant.8.clone.refs_2_) | copy-start | bytes 5620
  98.2 10.6 %copy-start.10 = (s32[1,81]{1,0:T(1,128)S(1)}, s32[1,81]{1,0:T(1,128)}, u32[]{:S(2)}) copy-start(s32[1,81]{1,0:T(1,128)} %constant.7.clone.refs_1_) | copy-start | bytes 976
  (2 other events, 4.1 us)
